TPU v7x, 32 devices: a whole 2x2x4 slice. The times are simulated.
32 devices in a mesh: grp: 4 (over x, core), blk: 4 (over z), sub: 2 (over y).
Axes of the slice: x: 2, y: 2, z: 4, core: 2. Of those that a mesh axis runs over, the one named last changes fastest.
Arguments:
- clips: bfloat16 [512, 128, 512], P(('grp', 'blk', 'sub')), may hold values from -6 to 6
- lengths: int32 [512], P(('grp', 'blk', 'sub')), may hold values from 32 to 128, as said below
- assign: int32 [16, 32], P(('grp', 'blk'), 'sub'), may hold values from 0 to 31, each once within a row
- text: bfloat16 [512, 1024], P(('grp', 'blk', 'sub')), may hold values from -6 to 6
- positives: int32 [4, 128], P('grp', ('blk', 'sub')), may hold values from 0 to 127, each once within a row
- conv_w: bfloat16 [1536, 512], replicated, may hold values from -0.15625 to 0.15625
- proj_w: bfloat16 [512, 1024], replicated, may hold values from -0.25 to 0.25
- logit_scale: float32 [], replicated, may hold values from 4 to 12
- logit_bias: float32 [], replicated, may hold values from -3 to -1
Outputs:
- audio_grad: float32 [512, 1024], P(('grp', 'blk', 'sub'))
- text_grad: float32 [512, 1024], P(('grp', 'blk', 'sub'))
Inputs may be any that keep to these rules, and one draw needn't show every extreme that they name: `lengths`: frames at or beyond a clip's length are padding; some clip has 128 frames. `assign`: each row lists each of its pair's 2 * 16 clips once; the first device of the pair takes the first 16 entries. `positives`: each row is a permutation: every text of a group is the match of exactly one audio slot of that group.
All inputs are finite; a program needn't handle non-finite values.
Results may differ from a plain program's by a relative error of at most 0.0045.
Values may be sent and summed in bfloat16 or wider, within the bound.
No kernel may reach another device: no remote copies, remote signals or barrier semaphores. Data moves between devices by JAX's collectives and lax.ppermute only.
A program may use at most 64 MiB of HBM per device.

v0:
```python
import jax
import jax.numpy as jnp
from jax import lax
from jax.sharding import PartitionSpec as P


def passed_along(block, axis, distance):
    devices = range(lax.axis_size(axis))
    route = [((i - distance) % len(devices), i) for i in devices]
    return lax.ppermute(block, axis, route)


def tower(clips, lengths, conv_w, proj_w):
    count_frames = clips.shape[1]
    half = count_frames // 2
    frame_ids = jnp.arange(count_frames, dtype=jnp.int32)
    inside = (frame_ids[None, :] < lengths[:, None])[:, :, None]
    kept = jnp.where(inside, clips, jnp.zeros((), clips.dtype))
    padded = jnp.pad(kept, ((0, 0), (1, 0), (0, 0)))
    stacked = jnp.concatenate(
        [
            padded[:, 0:count_frames:2],
            padded[:, 1:count_frames:2],
            padded[:, 2 : count_frames + 1 : 2],
        ],
        axis=2,
    )
    hidden = jax.nn.gelu(
        jnp.dot(stacked.reshape(-1, stacked.shape[2]), conv_w, preferred_element_type=jnp.float32)
    )
    hidden = hidden.reshape(clips.shape[0], half, -1)
    out_ids = jnp.arange(half, dtype=jnp.int32)
    valid = (2 * out_ids[None, :] < lengths[:, None])[:, :, None]
    counts = ((lengths + 1) // 2).astype(jnp.float32)
    pooled = (
        jnp.sum(jnp.where(valid, hidden, jnp.zeros((), hidden.dtype)), axis=1) / counts[:, None]
    ).astype(jnp.bfloat16)
    projected = jnp.dot(pooled, proj_w, preferred_element_type=jnp.float32)
    return (
        projected * lax.rsqrt(jnp.sum(projected * projected, axis=1, keepdims=True) + 1e-06)
    ).astype(jnp.bfloat16)


def normalize(values):
    wide = values.astype(jnp.float32)
    return (wide * lax.rsqrt(jnp.sum(wide * wide, axis=1, keepdims=True) + 1e-06)).astype(
        jnp.bfloat16
    )


def left_product(weights, block):
    return lax.dot_general(
        weights, block, (((0,), (0,)), ((), ())), preferred_element_type=jnp.float32
    )


def on_device(clips, lengths, assign, text, positives, conv_w, proj_w, logit_scale, logit_bias):
    slots = assign[0]
    own_embed = tower(clips, lengths, conv_w, proj_w)
    audio = lax.all_gather(own_embed, "sub", axis=0, tiled=True)[slots]
    own_text = normalize(text)
    group_text = lax.all_gather(own_text, ("blk", "sub"), axis=0, tiled=True)
    prev_text = passed_along(group_text, "grp", 1)
    group_rows = group_text.shape[0]
    width = group_text.shape[1]
    own_logits = (
        logit_scale
        * lax.dot_general(
            audio, group_text, (((1,), (1,)), ((), ())), preferred_element_type=jnp.float32
        )
        + logit_bias
    )
    next_logits = (
        logit_scale
        * lax.dot_general(
            audio, prev_text, (((1,), (1,)), ((), ())), preferred_element_type=jnp.float32
        )
        + logit_bias
    )
    hit = jnp.arange(group_rows, dtype=jnp.int32)[None, :] == positives[0][:, None]
    own_weights = jnp.where(hit, -jax.nn.sigmoid(-own_logits), jax.nn.sigmoid(own_logits)).astype(
        jnp.bfloat16
    )
    next_weights = jax.nn.sigmoid(next_logits).astype(jnp.bfloat16)
    audio_grad = logit_scale * (
        jnp.dot(own_weights, group_text, preferred_element_type=jnp.float32)
        + jnp.dot(next_weights, prev_text, preferred_element_type=jnp.float32)
    )
    summed = lax.psum_scatter(
        logit_scale
        * jnp.concatenate(
            [left_product(own_weights, audio), left_product(next_weights, audio)], axis=1
        ),
        ("blk", "sub"),
        scatter_dimension=0,
        tiled=True,
    )
    own_part = summed[:, :width]
    next_part = summed[:, width:]
    text_grad = own_part + passed_along(next_part, "grp", -1)
    return (audio_grad, text_grad)


def solution(mesh):
    in_specs = (
        P(("grp", "blk", "sub"), None, None),
        P(("grp", "blk", "sub")),
        P(("grp", "blk"), "sub"),
        P(("grp", "blk", "sub"), None),
        P("grp", ("blk", "sub")),
        P(),
        P(),
        P(),
        P(),
    )
    out_specs = (P(("grp", "blk", "sub"), None), P(("grp", "blk", "sub"), None))
    return jax.shard_map(
        on_device, mesh=mesh, in_specs=in_specs, out_specs=out_specs, check_vma=False
    )
```

profile of v0, /device:TPU:0, one launch (start us, length us, event | category | flops | bytes accessed | tf_op | source)
XLA Modules:
  0.0 162.9 jit_solution(16838572503940600882)
XLA Ops:
  7.2 0.0 copy-start
  7.2 0.0 reduce-scatter.2.cloned.1.call-start
  7.2 1.0 fusion.15
  8.2 0.8 fusion.16
  9.1 32.5 %all_gather.7 = bf16[128,1024]{1,0:T(8,128)(2,1)S(1)} all-gather(bf16[16,1024]{1,0:T(8,128)(2,1)S(1)} %fusion.16), channel_id=1, replica_groups=mesh['grp'=4,'blk'=4,'sub'=2] {'blk','sub'}, dimensions={0}, use_global_device_ids=true | all-gather | bytes 294912 | tf_op jit(solution)/shard_map/all_gather | solution.py:62
  41.6 0.0 collective-permute-start
  41.6 0.7 iota_compare_fusion
  42.3 1.8 %broadcast_select_fusion = bf16[16,128,512]{2,1,0:T(8,128)(2,1)S(1)} fusion(bf16[16,128,512]{2,1,0:T(8,128)(2,1)} %param.9, pred[16,128]{1,0:T(8,128)(4,1)S(1)} %iota_compare_fusion), kind=kLoop, calls=%fused_computation.11 | loop fusion | flops 1048576 | bytes 4196352 | tf_op jit(solution)/shard_map/jit(_where)/select_n | solution.py:18
  44.1 2.3 %pad.4 = bf16[16,129,512]{2,1,0:T(8,128)(2,1)} pad(bf16[16,128,512]{2,1,0:T(8,128)(2,1)S(1)} %broadcast_select_fusion, bf16[]{:T(256)} %constant.14.clone.1), padding=0_0x1_0x0_0 | pad | bytes 4210690 | tf_op jit(solution)/shard_map/jit(_pad)/pad | solution.py:19
  46.4 7.9 %slice.15 = bf16[16,64,512]{2,1,0:T(8,128)(2,1)S(1)} slice(bf16[16,129,512]{2,1,0:T(8,128)(2,1)} %pad.4), slice={[0:16:1], [0:128:2], [0:512:1]} | slice | bytes 2097152 | tf_op jit(solution)/shard_map/slice | solution.py:22
  54.3 0.0 copy-start.2
  54.3 9.5 %slice.16 = bf16[16,64,512]{2,1,0:T(8,128)(2,1)} slice(bf16[16,129,512]{2,1,0:T(8,128)(2,1)} %pad.4), slice={[0:16:1], [1:128:2], [0:512:1]} | slice | bytes 2097152 | tf_op jit(solution)/shard_map/slice | solution.py:23
  63.9 9.7 %slice.17 = bf16[16,64,512]{2,1,0:T(8,128)(2,1)} slice(bf16[16,129,512]{2,1,0:T(8,128)(2,1)} %pad.4), slice={[0:16:1], [2:129:2], [0:512:1]} | slice | bytes 2097152 | tf_op jit(solution)/shard_map/slice | solution.py:24
  73.5 0.0 copy-done.2
  73.6 0.1 broadcast_compare_fusion
  73.6 1.7 %pad_maximum_fusion = bf16[16,64,1536]{2,1,0:T(8,128)(2,1)S(1)} fusion(bf16[16,64,512]{2,1,0:T(8,128)(2,1)} %slice.17, bf16[16,64,512]{2,1,0:T(8,128)(2,1)} %slice.16, bf16[16,64,512]{2,1,0:T(8,128)(2,1)S(1)} %slice.15), kind=kLoop, calls=%fused_computation.1 | loop fusion | flops 9437184 | bytes 6291456 | tf_op jit(solution)/shard_map/concatenate | solution.py:20
  75.3 0.0 copy-done
  75.3 0.0 copy-start.1
  75.3 0.0 copy-start.3
  75.3 0.0 copy-start.4
  75.4 2.3 %select_reduce_fusion = f32[16,512]{1,0:T(8,128)S(1)} fusion(pred[16,64]{1,0:T(8,128)(4,1)S(1)} %broadcast_compare_fusion, bf16[1024,1536]{1,0:T(8,128)(2,1)S(1)} %bitcast.23, bf16[1536,512]{1,0:T(8,128)(2,1)S(1)} %copy-done), kind=kOutput, calls=%fused_computation.10 | convolution fusion | flops 1615847424 | bytes 4752384 | tf_op jit(solution)/shard_map/dot_general | solution.py:29
  77.7 0.0 copy-done.1
  77.7 0.4 multiply_reduce_fusion
  78.1 0.1 multiply_convert_fusion
  78.2 4.6 %all_gather.6 = bf16[32,1024]{1,0:T(8,128)(2,1)S(1)} all-gather(bf16[16,1024]{1,0:T(8,128)(2,1)S(1)} %multiply_convert_fusion), channel_id=1, replica_groups=mesh['grp'=4,'blk'=4,'sub'=2] {'sub'}, dimensions={0}, use_global_device_ids=true | all-gather | bytes 98304 | tf_op jit(solution)/shard_map/all_gather | solution.py:60
  82.8 0.0 copy-done.3
  84.1 0.6 gather_fusion
  84.7 0.0 copy-done.4
  84.7 0.2 select_convert_fusion
  84.9 0.2 fusion.22
  85.2 0.0 collective-permute-done
  85.2 0.2 fusion.14
  85.4 0.2 fusion.23
  85.6 1.1 maximum_multiply_fusion
  86.7 0.0 reduce-scatter.2.cloned.1.call-update
  86.7 0.2 fusion.21
  86.9 64.9 %reduce-scatter.2.cloned.1.call-done = f32[16,2048]{1,0:T(8,128)} async-done(((f32[128,2048]{1,0:T(8,128)}), f32[16,2048]{1,0:T(8,128)}) %reduce-scatter.2.cloned.1.call-update) | async-done | bytes 131088 | tf_op jit(solution)/shard_map/reduce_scatter | solution.py:89
  151.8 0.8 slice.23
  152.7 0.0 collective-permute-start.1
  152.7 0.8 fusion.7
  153.4 1.1 collective-permute-done.1
  154.6 1.5 slice_add_fusion
  (6 shorter events, 0.0 us)
Async XLA Ops:
  7.2 68.2 %copy-start = (bf16[1536,512]{1,0:T(8,128)(2,1)S(1)}, bf16[1536,512]{1,0:T(8,128)(2,1)}, u32[]{:S(2)}) copy-start(bf16[1536,512]{1,0:T(8,128)(2,1)} %param.14) | copy-start | bytes 4718596
  7.2 144.6 %reduce-scatter.2.cloned.1.call-start = ((), (), s32[]{:S(2)}) async-start(), calls=%async_computation.1 | async-start | bytes 1179648 | tf_op jit(solution)/shard_map/reduce_scatter | solution.py:89
  41.6 43.6 %collective-permute-start = (bf16[128,1024]{1,0:T(8,128)(2,1)S(1)}, bf16[128,1024]{1,0:T(8,128)(2,1)S(1)}, u32[]{:S(2)}, u32[]{:S(2)}) collective-permute-start(bf16[128,1024]{1,0:T(8,128)(2,1)S(1)} %all_gather.7), channel_id=1, source_target_pairs={{24,0},{0,8},{8,16},{16,24},{25,1},{1,9},{9,17},{17,25},{26,2},{2,... | collective-permute-start | bytes 786440 | tf_op jit(solution)/shard_map/ppermute | solution.py:10
  54.3 19.2 %copy-start.2 = (s32[16]{0:T(128)S(1)}, s32[16]{0:T(128)}, u32[]{:S(2)}) copy-start(s32[16]{0:T(128)} %param.10) | copy-start | bytes 196
  75.3 2.4 %copy-start.1 = (bf16[512,1024]{1,0:T(8,128)(2,1)S(1)}, bf16[512,1024]{1,0:T(8,128)(2,1)}, u32[]{:S(2)}) copy-start(bf16[512,1024]{1,0:T(8,128)(2,1)} %param.15) | copy-start | bytes 3145732
  75.3 7.5 %copy-start.3 = (s32[1,16]{1,0:T(1,128)S(1)}, s32[1,16]{1,0:T(1,128)}, u32[]{:S(2)}) copy-start(s32[1,16]{1,0:T(1,128)} %param.11) | copy-start | bytes 196
  75.3 9.4 %copy-start.4 = (s32[1,16]{1,0:T(1,128)S(1)}, s32[1,16]{1,0:T(1,128)}, u32[]{:S(2)}) copy-start(s32[1,16]{1,0:T(1,128)} %param.13) | copy-start | bytes 196
  152.7 1.9 %collective-permute-start.1 = (f32[16,1024]{1,0:T(8,128)S(1)}, f32[16,1024]{1,0:T(8,128)S(1)}, u32[]{:S(2)}, u32[]{:S(2)}) collective-permute-start(f32[16,1024]{1,0:T(8,128)S(1)} %slice.23), channel_id=1, source_target_pairs={{8,0},{16,8},{24,16},{0,24},{9,1},{17,9},{25,17},{1,25},{10,2},{18... | collective-permute-start | bytes 196616 | tf_op jit(solution)/shard_map/ppermute | solution.py:10
Sparse Core Ops, SparseCore 0:
  86.9 64.9 reduce-scatter.1
where the time goes:
time: 165 us; the launch traced here: 163 us
  waiting for transfers between devices  66.1 us (40%)
  blocking collectives  37.1 us (22%)
  local copies, waits for them, and re-layouts  30.9 us (19%)
  between operations  15.5 us (9%)
  other arithmetic  8.74 us (5%)
  matrix products  4.56 us (3%)
    reduce_scatter x1, waiting for transfers between devices, on_device(): lax.psum_scatter(logit_scale * jnp.concatenate([left_product(own_weights,...  64.9 us
    all_gather x1, blocking collectives, on_device(): group_text = lax.all_gather(own_text, ('blk', 'sub'), axis=0, tiled=True)  32.5 us
    slice x1, local copies, waits for them, and re-layouts, tower(): padded[:, 2:count_frames + 1:2]  9.68 us
    slice x1, local copies, waits for them, and re-layouts, tower(): padded[:, 1:count_frames:2]  9.54 us
    slice x1, local copies, waits for them, and re-layouts, tower(): padded[:, 0:count_frames:2]  7.93 us
    all_gather x1, blocking collectives, on_device(): audio = lax.all_gather(own_embed, 'sub', axis=0, tiled=True)[slots]  4.59 us
  transfers between devices with their start and end apart: 3, of which 2 were waited for; matrix products, arithmetic and copies ran while one was open for 24% of the time, Pallas kernels for 0%

commit v1 on v0

v1 whole, which is shorter than its diff:
```python
import functools

import jax
import jax.numpy as jnp
from jax import lax
from jax.experimental import pallas as pl
from jax.experimental.pallas import tpu as pltpu
from jax.sharding import PartitionSpec as P

BF16 = jnp.bfloat16
F32 = jnp.float32
LANES = 128
SMEM = pl.BlockSpec(memory_space=pltpu.SMEM)
VMEM = pl.BlockSpec(memory_space=pltpu.VMEM)
PARAMS = pltpu.CompilerParams(vmem_limit_bytes=48 * 2**20)


def swapped(block, axis, bit):
    devices = range(lax.axis_size(axis))
    return lax.ppermute(block, axis, [(i, i ^ bit) for i in devices])


def passed_along(block, axis, distance):
    devices = range(lax.axis_size(axis))
    return lax.ppermute(block, axis, [((i - distance) % len(devices), i) for i in devices])


def bits_of(size):
    assert size & (size - 1) == 0
    return [1 << k for k in reversed(range(size.bit_length() - 1))]


def doubled(block, axis, bits):
    for bit in bits:
        block = jnp.concatenate([block, swapped(block, axis, bit)], axis=0)
    return block


def gelu(x):
    return x * (0.5 + 0.5 * jnp.tanh(x * (0.7978845608028654 + 0.035677408136300125 * (x * x))))


def as_column(row):
    size = row.shape[1]
    at = lax.broadcasted_iota(jnp.int32, (size, size), 0)
    lane = lax.broadcasted_iota(jnp.int32, (size, size), 1)
    return jnp.sum(jnp.where(at == lane, jnp.broadcast_to(row, (size, size)), 0.0), 1, keepdims=True)


def as_row(column):
    size = column.shape[0]
    at = lax.broadcasted_iota(jnp.int32, (size, size), 0)
    lane = lax.broadcasted_iota(jnp.int32, (size, size), 1)
    return jnp.sum(jnp.where(at == lane, jnp.broadcast_to(column, (size, size)), 0.0), 0, keepdims=True)


def product(a, b, b_axis=0):
    return lax.dot_general(a, b, (((1,), (b_axis,)), ((), ())), preferred_element_type=F32)


def tower_kernel(lengths, clips, assign, positives, conv_w, out, wide, stacked):
    count, frames, channels = clips.shape
    half = frames // 2
    rows = lax.broadcasted_iota(jnp.int32, (half, 1), 0)
    wide[:, :, 0:8, :] = jnp.zeros((wide.shape[0], channels // LANES, 8, LANES), F32)
    for c in range(count):
        inside = 2 * rows + 1 < lengths[c]
        base = c * half
        buffer = wide.at[c % wide.shape[0]]
        for k in range(channels // LANES):
            buffer[k, 8 : 8 + frames, :] = clips[c, :, k * LANES : (k + 1) * LANES].astype(F32)
        for k in range(channels // LANES):
            strip = buffer.at[k]
            taps = (
                strip[pl.ds(7, half, stride=2), :],
                strip[pl.ds(8, half, stride=2), :],
                jnp.where(inside, strip[pl.ds(9, half, stride=2), :], 0.0),
            )
            for tap, values in enumerate(taps):
                first = tap * channels + k * LANES
                stacked[base : base + half, first : first + LANES] = values.astype(BF16)
    hidden = gelu(product(stacked[...], conv_w[...]))
    pooled = []
    for c in range(count):
        valid = 2 * rows < lengths[c]
        total = jnp.sum(
            jnp.where(valid, hidden[c * half : (c + 1) * half], 0.0), axis=0, keepdims=True
        )
        pooled.append(total / ((lengths[c] + 1) // 2).astype(F32))
    out[:, 0:channels] = jnp.concatenate(pooled, axis=0).astype(BF16)
    slots = as_column(assign[...].astype(F32))
    low = as_column((positives[...] & 255).astype(F32))
    high = as_column((positives[...] >> 8).astype(F32))
    lane = lax.broadcasted_iota(jnp.int32, (count, LANES), 1)
    marks = jnp.where(lane == 0, slots, jnp.where(lane == 1, low, jnp.where(lane == 2, high, 0.0)))
    out[:, channels : channels + LANES] = marks.astype(BF16)


def normalized(wide):
    return (wide * lax.rsqrt(jnp.sum(wide * wide, axis=1, keepdims=True) + 1e-06)).astype(BF16)


def weights(logits, hit):
    return jnp.where(hit, -jax.nn.sigmoid(-logits), jax.nn.sigmoid(logits)).astype(BF16)


def logits_kernel(
    bits, place, scale, bias, gathered, proj_w, texts, next_out, peer_out, text_out, audio_out
):
    channels = proj_w.shape[0]
    rows = gathered.shape[0]
    count = text_out.shape[0]
    blk, sub = place[0], place[1]
    ls, lb = scale[0], bias[0]
    marks = gathered[:, channels : channels + LANES].astype(F32)
    slot = marks[:, 0:1].astype(jnp.int32)
    match = marks[:, 1:2] + 256.0 * marks[:, 2:3]
    here = lax.broadcasted_iota(jnp.int32, (rows, 1), 0)
    other = jnp.where(slot < count, slot + count, slot - count)
    source = here // (2 * count) * (2 * count) + jnp.where(sub == 1, other, slot)
    lane = lax.broadcasted_iota(jnp.int32, (rows, rows), 1)
    pick = jnp.where(lane == source, 1.0, 0.0).astype(BF16)
    pooled = product(pick, gathered[:, 0:channels]).astype(BF16)
    audio = normalized(product(pooled, proj_w[...]))
    zt = normalized(texts[...].astype(F32))

    near = zt[0 : 2 * count]
    logits = ls * product(near, audio, 1) + lb
    at = lax.broadcasted_iota(jnp.int32, (2 * count, 1), 0)
    wanted = jnp.where(at < count, (blk * 2 + sub) * count + at, -1).astype(F32)
    pulled = ls * product(weights(logits, wanted == as_row(match)), audio)
    next_out[...] = pulled[count:].astype(BF16)
    text_out[...] = pulled[:count]

    pair = audio[0 : 2 * count]
    logits = ls * product(pair, zt, 1) + lb
    column = lax.broadcasted_iota(jnp.int32, (1, zt.shape[0]), 1)
    step = column // count
    away = jnp.zeros_like(column)
    for k, bit in enumerate(bits):
        away = away + ((step >> (k + 1)) & 1) * bit
    wanted = jnp.where((step & 1) == 0, ((blk ^ away) * 2 + sub) * count + column % count, -1)
    pushed = ls * product(weights(logits, wanted.astype(F32) == match[0 : 2 * count]), zt)
    peer_out[...] = pushed[count:].astype(BF16)
    audio_out[...] = pushed[:count]


def sum_kernel(audio, peer, text, after, audio_grad, text_grad):
    audio_grad[...] = audio[...] + peer[...].astype(F32)
    text_grad[...] = text[...] + after[...].astype(F32)


def on_device(clips, lengths, assign, text, positives, conv_w, proj_w, logit_scale, logit_bias):
    count, frames, channels = clips.shape
    width = text.shape[1]
    assert lax.axis_size("sub") == 2 and count <= 128
    bits = bits_of(lax.axis_size("blk"))
    texts = jnp.concatenate([text, passed_along(text, "grp", 1)], axis=0)
    texts = doubled(texts, "blk", bits)
    own = pl.pallas_call(
        tower_kernel,
        out_shape=jax.ShapeDtypeStruct((count, channels + LANES), BF16),
        in_specs=[SMEM, VMEM, VMEM, VMEM, VMEM],
        out_specs=VMEM,
        scratch_shapes=[
            pltpu.VMEM((2, channels // LANES, 8 + frames, LANES), F32),
            pltpu.VMEM((count * frames // 2, 3 * channels), BF16),
        ],
        compiler_params=PARAMS,
        cost_estimate=pl.CostEstimate(flops=count * frames * 3 * channels * channels, bytes_accessed=clips.size * 4, transcendentals=count * frames * channels // 2),
        name="tower",
    )(lengths, clips, assign, positives, conv_w)
    gathered = doubled(doubled(own, "sub", [1]), "blk", bits)
    place = jnp.stack([lax.axis_index("blk"), lax.axis_index("sub")]).astype(jnp.int32)
    block = (count, width)
    after, peer, text_part, audio_part = pl.pallas_call(
        functools.partial(logits_kernel, bits),
        out_shape=[jax.ShapeDtypeStruct(block, t) for t in (BF16, BF16, F32, F32)],
        in_specs=[SMEM, SMEM, SMEM, VMEM, VMEM, VMEM],
        out_specs=[VMEM] * 4,
        compiler_params=PARAMS,
        name="logits",
    )(place, logit_scale.reshape(1), logit_bias.reshape(1), gathered, proj_w, texts)
    after = passed_along(after, "grp", -1)
    peer = swapped(peer, "sub", 1)
    return pl.pallas_call(
        sum_kernel,
        out_shape=[jax.ShapeDtypeStruct(block, F32)] * 2,
        in_specs=[VMEM] * 4,
        out_specs=[VMEM] * 2,
        compiler_params=PARAMS,
        name="sums",
    )(audio_part, peer, text_part, after)


def solution(mesh):
    in_specs = (
        P(("grp", "blk", "sub"), None, None),
        P(("grp", "blk", "sub")),
        P(("grp", "blk"), "sub"),
        P(("grp", "blk", "sub"), None),
        P("grp", ("blk", "sub")),
        P(),
        P(),
        P(),
        P(),
    )
    out_specs = (P(("grp", "blk", "sub"), None), P(("grp", "blk", "sub"), None))
    return jax.shard_map(
        on_device, mesh=mesh, in_specs=in_specs, out_specs=out_specs, check_vma=False
    )
```

time: 165 us -> 34.7 us (0.21)
  waiting for transfers between devices: 66.1 us -> 7.9 us
  blocking collectives: 37.1 us -> 0 us
  local copies, waits for them, and re-layouts: 30.9 us -> 4.97 us
  between operations: 15.5 us -> 2.01 us
  starting transfers between devices: 0.04 us -> 13.1 us
  other arithmetic: 8.74 us -> 0.14 us
  Pallas kernels: 0 us -> 6 us
  matrix products: 4.56 us -> 0 us
    reduce_scatter x1 -> x0, waiting for transfers between devices: 64.9 us -> none  [on_device(): lax.psum_scatter(logit_scale * jnp.concatenate([left_product(own_weights,...]
    all_gather x2 -> x0, blocking collectives: 37.1 us -> none  [the longest x1 32.5 us: on_device(): group_text = lax.all_gather(own_text, ('blk', 'sub'), axis=0, tiled=True)]
    slice x4 -> x0, local copies, waits for them, and re-layouts: 28 us -> none  [the longest x1 9.68 us: tower(): padded[:, 2:count_frames + 1:2]]
    ppermute x2 -> x8, starting transfers between devices: 0.01 us -> 13.1 us  [the longest x6 13.1 us: swapped(): return lax.ppermute(block, axis, [(i, i ^ bit) for i in devices])]
    ppermute x2 -> x8, waiting for transfers between devices: 1.12 us -> 7.9 us  [the longest x6 7.9 us: swapped(): return lax.ppermute(block, axis, [(i, i ^ bit) for i in devices])]
    pallas_call x0 -> x3, Pallas kernels: none -> 6 us  [the longest x1 3.48 us: on_device(): pl.pallas_call(tower_kernel, out_shape=jax.ShapeDtypeStruct((count, chann...]
    unnamed x10 -> x14, local copies, waits for them, and re-layouts: 0.03 us -> 4.97 us
    dot_general x8 -> x0, matrix products: 4.56 us -> none  [the longest x1 2.34 us: tower(): jnp.dot(stacked.reshape(-1, stacked.shape[2]), conv_w, preferred_element_...]
  transfers between devices with their start and end apart: 3 -> 8, of which waited for: 2 -> 5; matrix products, arithmetic and copies ran while one was open for 24% -> 0% of each run, Pallas kernels for 0% -> 0%
where the time goes in v1:
time: 34.7 us; the launch traced here: 34.1 us
  starting transfers between devices  13.1 us (38%)
  waiting for transfers between devices  7.9 us (23%)
  Pallas kernels  6 us (17%)
  local copies, waits for them, and re-layouts  4.97 us (14%)
  between operations  2.01 us (6%)
    ppermute x6, starting transfers between devices, swapped(): return lax.ppermute(block, axis, [(i, i ^ bit) for i in devices])  13.1 us
    ppermute x6, waiting for transfers between devices, swapped(): return lax.ppermute(block, axis, [(i, i ^ bit) for i in devices])  7.9 us
    unnamed x14, local copies, waits for them, and re-layouts  4.97 us
    pallas_call x1, Pallas kernels, on_device(): pl.pallas_call(tower_kernel, out_shape=jax.ShapeDtypeStruct((count, chann...  3.48 us
    pallas_call x1, Pallas kernels, on_device(): pl.pallas_call(functools.partial(logits_kernel, bits), out_shape=[jax.Sha...  1.85 us
  transfers between devices with their start and end apart: 8, of which 5 were waited for; matrix products, arithmetic and copies ran while one was open for 0% of the time, Pallas kernels for 0%

profile of v1, /device:TPU:0, one launch (start us, length us, event | category | flops | bytes accessed | tf_op | source)
XLA Modules:
  0.0 34.1 jit_solution(9082730430789901415)
XLA Ops:
  0.6 0.0 copy-start.1
  0.6 1.6 %copy-done.1 = bf16[16,128,512]{2,1,0:T(8,128)(2,1)S(1)} copy-done((bf16[16,128,512]{2,1,0:T(8,128)(2,1)S(1)}, bf16[16,128,512]{2,1,0:T(8,128)(2,1)}, u32[]{:S(2)}) %copy-start.1) | copy-done | bytes 2097176
  2.2 0.0 copy-start.2
  2.2 1.4 %copy-done.2 = bf16[1536,512]{1,0:T(8,128)(2,1)S(1)} copy-done((bf16[1536,512]{1,0:T(8,128)(2,1)S(1)}, bf16[1536,512]{1,0:T(8,128)(2,1)}, u32[]{:S(2)}) %copy-start.2) | copy-done | bytes 1572888
  3.6 0.0 copy-start.3
  3.6 0.7 %copy-done.3 = s32[16]{0:T(128)S(1)} copy-done((s32[16]{0:T(128)S(1)}, s32[16]{0:T(128)}, u32[]{:S(2)}) %copy-start.3) | copy-done | bytes 88
  4.3 0.0 copy-start.4
  4.3 0.7 %copy-done.4 = s32[1,16]{1,0:T(1,128)S(1)} copy-done((s32[1,16]{1,0:T(1,128)S(1)}, s32[1,16]{1,0:T(1,128)}, u32[]{:S(2)}) %copy-start.4) | copy-done | bytes 88
  4.9 0.0 copy-start.5
  4.9 0.7 %copy-done.5 = s32[1,16]{1,0:T(1,128)S(1)} copy-done((s32[1,16]{1,0:T(1,128)S(1)}, s32[1,16]{1,0:T(1,128)}, u32[]{:S(2)}) %copy-start.5) | copy-done | bytes 88
  5.6 0.0 copy-start.6
  5.6 3.5 %tower.1 = bf16[16,640]{1,0:T(8,128)(2,1)S(1)} custom-call(s32[16]{0:T(128)S(1)} %copy-done.3, bf16[16,128,512]{2,1,0:T(8,128)(2,1)S(1)} %copy-done.1, s32[1,16]{1,0:T(1,128)S(1)} %copy-done.4, s32[1,16]{1,0:T(1,128)S(1)} %copy-done.5, bf16[1536,512]{1,0:T(8,128)(2,1)S(1)} %copy-done.2), custom_call_target="tpu_custom_call" | custom-call | flops 1610612736 | bytes 4194304 | tf_op jit(solution)/shard_map/tower/pallas_call | solution.py:160
  9.1 0.0 copy-start
  9.1 3.0 %collective-permute-start = (bf16[16,640]{1,0:T(8,128)(2,1)S(1)}, bf16[16,640]{1,0:T(8,128)(2,1)S(1)}, u32[]{:S(2)}, u32[]{:S(2)}) collective-permute-start(bf16[16,640]{1,0:T(8,128)(2,1)S(1)} %tower.1), channel_id=1, source_target_pairs={{0,1},{1,0},{2,3},{3,2},{4,5},{5,4},{6,7},{7,6},{8,9},{9,8},{10,11... | collective-permute-start | bytes 61448 | tf_op jit(solution)/shard_map/ppermute | solution.py:20
  12.1 0.0 copy-done.6
  12.1 0.0 collective-permute-start.3
  12.1 1.8 %collective-permute-done = bf16[16,640]{1,0:T(8,128)(2,1)S(1)} collective-permute-done((bf16[16,640]{1,0:T(8,128)(2,1)S(1)}, bf16[16,640]{1,0:T(8,128)(2,1)S(1)}, u32[]{:S(2)}, u32[]{:S(2)}) %collective-permute-start) | collective-permute-done | bytes 20512 | tf_op jit(solution)/shard_map/ppermute | solution.py:20
  13.9 3.1 %collective-permute-start.1 = (bf16[32,640]{1,0:T(8,128)(2,1)S(1)}, bf16[32,640]{1,0:T(8,128)(2,1)S(1)}, u32[]{:S(2)}, u32[]{:S(2)}) collective-permute-start(bf16[32,640]{1,0:T(8,128)(2,1)S(1)} %pad_maximum_fusion.5), channel_id=1, source_target_pairs={{0,4},{2,6},{4,0},{6,2},{1,5},{3,7},{5,1},{7,3},{8,12},{10,14},{12... | collective-permute-start | bytes 122888 | tf_op jit(solution)/shard_map/ppermute | solution.py:20
  17.0 0.0 collective-permute-done.3
  17.0 1.1 %collective-permute-start.4 = (bf16[32,1024]{1,0:T(8,128)(2,1)S(1)}, bf16[32,1024]{1,0:T(8,128)(2,1)S(1)}, u32[]{:S(2)}, u32[]{:S(2)}) collective-permute-start(bf16[32,1024]{1,0:T(8,128)(2,1)S(1)} %pad_maximum_fusion.4), channel_id=1, source_target_pairs={{0,4},{2,6},{4,0},{6,2},{1,5},{3,7},{5,1},{7,3},{8,12},{10,14},{12... | collective-permute-start | bytes 196616 | tf_op jit(solution)/shard_map/ppermute | solution.py:20
  18.1 1.1 %collective-permute-done.1 = bf16[32,640]{1,0:T(8,128)(2,1)S(1)} collective-permute-done((bf16[32,640]{1,0:T(8,128)(2,1)S(1)}, bf16[32,640]{1,0:T(8,128)(2,1)S(1)}, u32[]{:S(2)}, u32[]{:S(2)}) %collective-permute-start.1) | collective-permute-done | bytes 40992 | tf_op jit(solution)/shard_map/ppermute | solution.py:20
  19.2 2.0 %collective-permute-start.2 = (bf16[64,640]{1,0:T(8,128)(2,1)S(1)}, bf16[64,640]{1,0:T(8,128)(2,1)S(1)}, u32[]{:S(2)}, u32[]{:S(2)}) collective-permute-start(bf16[64,640]{1,0:T(8,128)(2,1)S(1)} %pad_maximum_fusion.3), channel_id=1, source_target_pairs={{0,2},{2,0},{4,6},{6,4},{1,3},{3,1},{5,7},{7,5},{8,10},{10,8},{12,... | collective-permute-start | bytes 245768 | tf_op jit(solution)/shard_map/ppermute | solution.py:20
  21.2 1.1 %collective-permute-done.4 = bf16[32,1024]{1,0:T(8,128)(2,1)S(1)} collective-permute-done((bf16[32,1024]{1,0:T(8,128)(2,1)S(1)}, bf16[32,1024]{1,0:T(8,128)(2,1)S(1)}, u32[]{:S(2)}, u32[]{:S(2)}) %collective-permute-start.4) | collective-permute-done | bytes 65568 | tf_op jit(solution)/shard_map/ppermute | solution.py:20
  22.3 2.3 %collective-permute-start.5 = (bf16[64,1024]{1,0:T(8,128)(2,1)S(1)}, bf16[64,1024]{1,0:T(8,128)(2,1)S(1)}, u32[]{:S(2)}, u32[]{:S(2)}) collective-permute-start(bf16[64,1024]{1,0:T(8,128)(2,1)S(1)} %pad_maximum_fusion.2), channel_id=1, source_target_pairs={{0,2},{2,0},{4,6},{6,4},{1,3},{3,1},{5,7},{7,5},{8,10},{10,8},{12,... | collective-permute-start | bytes 393224 | tf_op jit(solution)/shard_map/ppermute | solution.py:20
  24.6 0.1 pad_add_fusion.place
  26.0 0.0 collective-permute-done.2
  26.0 1.5 %collective-permute-done.5 = bf16[64,1024]{1,0:T(8,128)(2,1)S(1)} collective-permute-done((bf16[64,1024]{1,0:T(8,128)(2,1)S(1)}, bf16[64,1024]{1,0:T(8,128)(2,1)S(1)}, u32[]{:S(2)}, u32[]{:S(2)}) %collective-permute-start.5) | collective-permute-done | bytes 131104 | tf_op jit(solution)/shard_map/ppermute | solution.py:20
  27.6 0.0 copy-done
  27.6 1.9 %logits.1 = (bf16[16,1024]{1,0:T(8,128)(2,1)S(1)}, bf16[16,1024]{1,0:T(8,128)(2,1)S(1)}, f32[16,1024]{1,0:T(8,128)S(1)}, f32[16,1024]{1,0:T(8,128)S(1)}) custom-call(s32[2]{0:T(128)S(1)} %pad_add_fusion.place, f32[1]{0:T(128)} %bitcast.4.scale, f32[1]{0:T(128)} %bitcast.5.bias, bf16[128,640]{1,0:T(8,128)(2,1)S(1)} %pad_maximum_fusion.1.gathered, ...), custom_call_target="tpu_custom_call" | custom-call | tf_op jit(solution)/shard_map/logits/pallas_call | solution.py:176
  29.4 1.6 %collective-permute-start.6 = (bf16[16,1024]{1,0:T(8,128)(2,1)S(1)}, bf16[16,1024]{1,0:T(8,128)(2,1)S(1)}, u32[]{:S(2)}, u32[]{:S(2)}) collective-permute-start(bf16[16,1024]{1,0:T(8,128)(2,1)S(1)} %get-tuple-element.7), channel_id=1, source_target_pairs={{0,1},{1,0},{2,3},{3,2},{4,5},{5,4},{6,7},{7,6},{8,9},{9,8},{10,11... | collective-permute-start | bytes 98312 | tf_op jit(solution)/shard_map/ppermute | solution.py:20
  31.0 0.0 collective-permute-start.7
  31.0 2.4 %collective-permute-done.6.peer = bf16[16,1024]{1,0:T(8,128)(2,1)S(1)} collective-permute-done((bf16[16,1024]{1,0:T(8,128)(2,1)S(1)}, bf16[16,1024]{1,0:T(8,128)(2,1)S(1)}, u32[]{:S(2)}, u32[]{:S(2)}) %collective-permute-start.6) | collective-permute-done | bytes 32800 | tf_op jit(solution)/shard_map/ppermute | solution.py:20
  33.4 0.0 collective-permute-done.7.after
  33.4 0.7 %sums.1 = (f32[16,1024]{1,0:T(8,128)}, f32[16,1024]{1,0:T(8,128)}) custom-call(f32[16,1024]{1,0:T(8,128)S(1)} %get-tuple-element.6.audio, bf16[16,1024]{1,0:T(8,128)(2,1)S(1)} %collective-permute-done.6.peer, f32[16,1024]{1,0:T(8,128)S(1)} %get-tuple-element.8.text, bf16[16,1024]{1,0:T(8,128)(2,1)S(1)} %collective-permute-done.7.after), custom_call_target="tpu_custom_call" | custom-call | tf_op jit(solution)/shard_map/sums/pallas_call | solution.py:186
  (6 shorter events, 0.1 us)
Async XLA Ops:
  0.6 1.6 %copy-start.1 = (bf16[16,128,512]{2,1,0:T(8,128)(2,1)S(1)}, bf16[16,128,512]{2,1,0:T(8,128)(2,1)}, u32[]{:S(2)}) copy-start(bf16[16,128,512]{2,1,0:T(8,128)(2,1)} %clips.1) | copy-start | bytes 6291460
  2.2 1.4 %copy-start.2 = (bf16[1536,512]{1,0:T(8,128)(2,1)S(1)}, bf16[1536,512]{1,0:T(8,128)(2,1)}, u32[]{:S(2)}) copy-start(bf16[1536,512]{1,0:T(8,128)(2,1)} %conv_w.1) | copy-start | bytes 4718596
  3.6 0.7 %copy-start.3 = (s32[16]{0:T(128)S(1)}, s32[16]{0:T(128)}, u32[]{:S(2)}) copy-start(s32[16]{0:T(128)} %lengths.1) | copy-start | bytes 196
  4.3 0.7 %copy-start.4 = (s32[1,16]{1,0:T(1,128)S(1)}, s32[1,16]{1,0:T(1,128)}, u32[]{:S(2)}) copy-start(s32[1,16]{1,0:T(1,128)} %assign.1) | copy-start | bytes 196
  4.9 0.7 %copy-start.5 = (s32[1,16]{1,0:T(1,128)S(1)}, s32[1,16]{1,0:T(1,128)}, u32[]{:S(2)}) copy-start(s32[1,16]{1,0:T(1,128)} %positives.1) | copy-start | bytes 196
  5.6 6.5 %copy-start.6 = (bf16[16,1024]{1,0:T(8,128)(2,1)S(1)}, bf16[16,1024]{1,0:T(8,128)(2,1)}, u32[]{:S(2)}) copy-start(bf16[16,1024]{1,0:T(8,128)(2,1)} %param.12) | copy-start | bytes 98308
  9.1 18.5 %copy-start = (bf16[512,1024]{1,0:T(8,128)(2,1)S(1)}, bf16[512,1024]{1,0:T(8,128)(2,1)}, u32[]{:S(2)}) copy-start(bf16[512,1024]{1,0:T(8,128)(2,1)} %proj_w.1) | copy-start | bytes 3145732
  9.1 4.8 %collective-permute-start = (bf16[16,640]{1,0:T(8,128)(2,1)S(1)}, bf16[16,640]{1,0:T(8,128)(2,1)S(1)}, u32[]{:S(2)}, u32[]{:S(2)}) collective-permute-start(bf16[16,640]{1,0:T(8,128)(2,1)S(1)} %tower.1), channel_id=1, source_target_pairs={{0,1},{1,0},{2,3},{3,2},{4,5},{5,4},{6,7},{7,6},{8,9},{9,8},{10,11... | collective-permute-start | bytes 61448 | tf_op jit(solution)/shard_map/ppermute | solution.py:20
  12.1 4.9 %collective-permute-start.3 = (bf16[16,1024]{1,0:T(8,128)(2,1)S(1)}, bf16[16,1024]{1,0:T(8,128)(2,1)S(1)}, u32[]{:S(2)}, u32[]{:S(2)}) collective-permute-start(bf16[16,1024]{1,0:T(8,128)(2,1)S(1)} %copy-done.6), channel_id=1, source_target_pairs={{24,0},{0,8},{8,16},{16,24},{25,1},{1,9},{9,17},{17,25},{26,2},{2,... | collective-permute-start | bytes 98312 | tf_op jit(solution)/shard_map/ppermute | solution.py:25
  13.9 5.3 %collective-permute-start.1 = (bf16[32,640]{1,0:T(8,128)(2,1)S(1)}, bf16[32,640]{1,0:T(8,128)(2,1)S(1)}, u32[]{:S(2)}, u32[]{:S(2)}) collective-permute-start(bf16[32,640]{1,0:T(8,128)(2,1)S(1)} %pad_maximum_fusion.5), channel_id=1, source_target_pairs={{0,4},{2,6},{4,0},{6,2},{1,5},{3,7},{5,1},{7,3},{8,12},{10,14},{12... | collective-permute-start | bytes 122888 | tf_op jit(solution)/shard_map/ppermute | solution.py:20
  17.0 5.2 %collective-permute-start.4 = (bf16[32,1024]{1,0:T(8,128)(2,1)S(1)}, bf16[32,1024]{1,0:T(8,128)(2,1)S(1)}, u32[]{:S(2)}, u32[]{:S(2)}) collective-permute-start(bf16[32,1024]{1,0:T(8,128)(2,1)S(1)} %pad_maximum_fusion.4), channel_id=1, source_target_pairs={{0,4},{2,6},{4,0},{6,2},{1,5},{3,7},{5,1},{7,3},{8,12},{10,14},{12... | collective-permute-start | bytes 196616 | tf_op jit(solution)/shard_map/ppermute | solution.py:20
  19.2 6.8 %collective-permute-start.2 = (bf16[64,640]{1,0:T(8,128)(2,1)S(1)}, bf16[64,640]{1,0:T(8,128)(2,1)S(1)}, u32[]{:S(2)}, u32[]{:S(2)}) collective-permute-start(bf16[64,640]{1,0:T(8,128)(2,1)S(1)} %pad_maximum_fusion.3), channel_id=1, source_target_pairs={{0,2},{2,0},{4,6},{6,4},{1,3},{3,1},{5,7},{7,5},{8,10},{10,8},{12,... | collective-permute-start | bytes 245768 | tf_op jit(solution)/shard_map/ppermute | solution.py:20
  22.3 5.3 %collective-permute-start.5 = (bf16[64,1024]{1,0:T(8,128)(2,1)S(1)}, bf16[64,1024]{1,0:T(8,128)(2,1)S(1)}, u32[]{:S(2)}, u32[]{:S(2)}) collective-permute-start(bf16[64,1024]{1,0:T(8,128)(2,1)S(1)} %pad_maximum_fusion.2), channel_id=1, source_target_pairs={{0,2},{2,0},{4,6},{6,4},{1,3},{3,1},{5,7},{7,5},{8,10},{10,8},{12,... | collective-permute-start | bytes 393224 | tf_op jit(solution)/shard_map/ppermute | solution.py:20
  29.4 4.0 %collective-permute-start.6 = (bf16[16,1024]{1,0:T(8,128)(2,1)S(1)}, bf16[16,1024]{1,0:T(8,128)(2,1)S(1)}, u32[]{:S(2)}, u32[]{:S(2)}) collective-permute-start(bf16[16,1024]{1,0:T(8,128)(2,1)S(1)} %get-tuple-element.7), channel_id=1, source_target_pairs={{0,1},{1,0},{2,3},{3,2},{4,5},{5,4},{6,7},{7,6},{8,9},{9,8},{10,11... | collective-permute-start | bytes 98312 | tf_op jit(solution)/shard_map/ppermute | solution.py:20
  31.0 2.4 %collective-permute-start.7 = (bf16[16,1024]{1,0:T(8,128)(2,1)S(1)}, bf16[16,1024]{1,0:T(8,128)(2,1)S(1)}, u32[]{:S(2)}, u32[]{:S(2)}) collective-permute-start(bf16[16,1024]{1,0:T(8,128)(2,1)S(1)} %get-tuple-element.9), channel_id=1, source_target_pairs={{8,0},{16,8},{24,16},{0,24},{9,1},{17,9},{25,17},{1,25},{10,2},{18... | collective-permute-start | bytes 98312 | tf_op jit(solution)/shard_map/ppermute | solution.py:25

commit v2 on v1

--- a/solution.py
+++ b/solution.py
@@ -12,6 +12,7 @@
 LANES = 128
 SMEM = pl.BlockSpec(memory_space=pltpu.SMEM)
 VMEM = pl.BlockSpec(memory_space=pltpu.VMEM)
+HBM = pl.BlockSpec(memory_space=pltpu.HBM)
 PARAMS = pltpu.CompilerParams(vmem_limit_bytes=48 * 2**20)
 
 
@@ -58,12 +59,29 @@
     return lax.dot_general(a, b, (((1,), (b_axis,)), ((), ())), preferred_element_type=F32)
 
 
-def tower_kernel(lengths, clips, assign, positives, conv_w, out, wide, stacked):
+def tower_kernel(
+    lengths_in, clips_in, assign_in, positives_in, conv_in, proj_in,
+    out, proj_w, lengths, clips, assign, positives, conv_w, wide, stacked, sems,
+):
     count, frames, channels = clips.shape
     half = frames // 2
+    parts = clips.shape[0] // 4
+    copies = [pltpu.make_async_copy(lengths_in, lengths, sems.at[0])]
+    for n in range(4):
+        part = pl.ds(n * parts, parts)
+        copies.append(pltpu.make_async_copy(clips_in.at[part], clips.at[part], sems.at[1 + n]))
+    copies.append(pltpu.make_async_copy(conv_in, conv_w, sems.at[5]))
+    copies.append(pltpu.make_async_copy(assign_in, assign, sems.at[6]))
+    copies.append(pltpu.make_async_copy(positives_in, positives, sems.at[7]))
+    copies.append(pltpu.make_async_copy(proj_in, proj_w, sems.at[8]))
+    for copy in copies:
+        copy.start()
+    wide[:, :, 0:8, :] = jnp.zeros((wide.shape[0], channels // LANES, 8, LANES), F32)
     rows = lax.broadcasted_iota(jnp.int32, (half, 1), 0)
-    wide[:, :, 0:8, :] = jnp.zeros((wide.shape[0], channels // LANES, 8, LANES), F32)
+    copies[0].wait()
     for c in range(count):
+        if c % parts == 0:
+            copies[1 + c // parts].wait()
         inside = 2 * rows + 1 < lengths[c]
         base = c * half
         buffer = wide.at[c % wide.shape[0]]
@@ -79,6 +97,8 @@
             for tap, values in enumerate(taps):
                 first = tap * channels + k * LANES
                 stacked[base : base + half, first : first + LANES] = values.astype(BF16)
+    for copy in copies[5:-1]:
+        copy.wait()
     hidden = gelu(product(stacked[...], conv_w[...]))
     pooled = []
     for c in range(count):
@@ -94,6 +114,7 @@
     lane = lax.broadcasted_iota(jnp.int32, (count, LANES), 1)
     marks = jnp.where(lane == 0, slots, jnp.where(lane == 1, low, jnp.where(lane == 2, high, 0.0)))
     out[:, channels : channels + LANES] = marks.astype(BF16)
+    copies[-1].wait()
 
 
 def normalized(wide):
@@ -104,43 +125,53 @@
     return jnp.where(hit, -jax.nn.sigmoid(-logits), jax.nn.sigmoid(logits)).astype(BF16)
 
 
-def logits_kernel(
-    bits, place, scale, bias, gathered, proj_w, texts, next_out, peer_out, text_out, audio_out
-):
+def text_kernel(scale, bias, gathered, proj_w, texts, after_out, text_out, pair_out):
     channels = proj_w.shape[0]
     rows = gathered.shape[0]
     count = text_out.shape[0]
-    blk, sub = place[0], place[1]
-    ls, lb = scale[0], bias[0]
+    column = rows // 2
+    blk, sub = lax.axis_index("blk"), lax.axis_index("sub")
+    scale, bias = scale[0], bias[0]
     marks = gathered[:, channels : channels + LANES].astype(F32)
     slot = marks[:, 0:1].astype(jnp.int32)
     match = marks[:, 1:2] + 256.0 * marks[:, 2:3]
     here = lax.broadcasted_iota(jnp.int32, (rows, 1), 0)
-    other = jnp.where(slot < count, slot + count, slot - count)
-    source = here // (2 * count) * (2 * count) + jnp.where(sub == 1, other, slot)
+    block = here % column // count
+    source = (slot // count ^ sub) * column + block * count + slot % count
     lane = lax.broadcasted_iota(jnp.int32, (rows, rows), 1)
     pick = jnp.where(lane == source, 1.0, 0.0).astype(BF16)
     pooled = product(pick, gathered[:, 0:channels]).astype(BF16)
     audio = normalized(product(pooled, proj_w[...]))
-    zt = normalized(texts[...].astype(F32))
-
-    near = zt[0 : 2 * count]
-    logits = ls * product(near, audio, 1) + lb
+    pair_out[0:count] = audio[0:count]
+    pair_out[count:] = audio[column : column + count]
+    zt = normalized(texts[0 : 2 * count].astype(F32))
+    logits = scale * product(zt, audio, 1) + bias
     at = lax.broadcasted_iota(jnp.int32, (2 * count, 1), 0)
     wanted = jnp.where(at < count, (blk * 2 + sub) * count + at, -1).astype(F32)
-    pulled = ls * product(weights(logits, wanted == as_row(match)), audio)
-    next_out[...] = pulled[count:].astype(BF16)
+    pulled = scale * product(weights(logits, wanted == as_row(match)), audio)
+    after_out[...] = pulled[count:].astype(BF16)
     text_out[...] = pulled[:count]
 
-    pair = audio[0 : 2 * count]
-    logits = ls * product(pair, zt, 1) + lb
-    column = lax.broadcasted_iota(jnp.int32, (1, zt.shape[0]), 1)
-    step = column // count
-    away = jnp.zeros_like(column)
+
+def audio_kernel(bits, scale, bias, pair, gathered, texts, peer_out, audio_out):
+    count = pair.shape[0] // 2
+    column = gathered.shape[0] // 2
+    channels = gathered.shape[1] - LANES
+    blk, sub = lax.axis_index("blk"), lax.axis_index("sub")
+    scale, bias = scale[0], bias[0]
+    marks = jnp.concatenate(
+        [gathered[0:count, channels:], gathered[column : column + count, channels:]], axis=0
+    ).astype(F32)
+    match = marks[:, 1:2] + 256.0 * marks[:, 2:3]
+    zt = normalized(texts[...].astype(F32))
+    logits = scale * product(pair[...], zt, 1) + bias
+    at = lax.broadcasted_iota(jnp.int32, (1, 2 * column), 1)
+    step = at // count
+    away = jnp.zeros_like(at)
     for k, bit in enumerate(bits):
         away = away + ((step >> (k + 1)) & 1) * bit
-    wanted = jnp.where((step & 1) == 0, ((blk ^ away) * 2 + sub) * count + column % count, -1)
-    pushed = ls * product(weights(logits, wanted.astype(F32) == match[0 : 2 * count]), zt)
+    wanted = jnp.where((step & 1) == 0, ((blk ^ away) * 2 + sub) * count + at % count, -1)
+    pushed = scale * product(weights(logits, wanted.astype(F32) == match), zt)
     peer_out[...] = pushed[count:].astype(BF16)
     audio_out[...] = pushed[:count]
 
@@ -150,38 +181,71 @@
     text_grad[...] = text[...] + after[...].astype(F32)
 
 
+def in_hbm(array):
+    return pltpu.with_memory_space_constraint(array, pltpu.HBM)
+
+
 def on_device(clips, lengths, assign, text, positives, conv_w, proj_w, logit_scale, logit_bias):
     count, frames, channels = clips.shape
     width = text.shape[1]
-    assert lax.axis_size("sub") == 2 and count <= 128
+    assert lax.axis_size("sub") == 2 and count <= 128 and count % 4 == 0
     bits = bits_of(lax.axis_size("blk"))
-    texts = jnp.concatenate([text, passed_along(text, "grp", 1)], axis=0)
-    texts = doubled(texts, "blk", bits)
-    own = pl.pallas_call(
+    before = passed_along(text, "grp", 1)
+    inputs = (lengths, clips, assign, positives, conv_w, proj_w)
+    own, proj_w = pl.pallas_call(
         tower_kernel,
-        out_shape=jax.ShapeDtypeStruct((count, channels + LANES), BF16),
-        in_specs=[SMEM, VMEM, VMEM, VMEM, VMEM],
-        out_specs=VMEM,
+        out_shape=[
+            jax.ShapeDtypeStruct((count, channels + LANES), BF16),
+            jax.ShapeDtypeStruct(proj_w.shape, BF16),
+        ],
+        in_specs=[HBM] * 6,
+        out_specs=[VMEM] * 2,
         scratch_shapes=[
+            pltpu.SMEM(lengths.shape, jnp.int32),
+            pltpu.VMEM(clips.shape, BF16),
+            pltpu.VMEM(assign.shape, jnp.int32),
+            pltpu.VMEM(positives.shape, jnp.int32),
+            pltpu.VMEM(conv_w.shape, BF16),
             pltpu.VMEM((2, channels // LANES, 8 + frames, LANES), F32),
             pltpu.VMEM((count * frames // 2, 3 * channels), BF16),
+            pltpu.SemaphoreType.DMA((9,)),
         ],
         compiler_params=PARAMS,
-        cost_estimate=pl.CostEstimate(flops=count * frames * 3 * channels * channels, bytes_accessed=clips.size * 4, transcendentals=count * frames * channels // 2),
+        cost_estimate=pl.CostEstimate(
+            flops=count * frames * 3 * channels * channels,
+            bytes_accessed=clips.size * 4,
+            transcendentals=count * frames * channels // 2,
+        ),
         name="tower",
-    )(lengths, clips, assign, positives, conv_w)
-    gathered = doubled(doubled(own, "sub", [1]), "blk", bits)
-    place = jnp.stack([lax.axis_index("blk"), lax.axis_index("sub")]).astype(jnp.int32)
+    )(*map(in_hbm, inputs))
+    own, both = lax.optimization_barrier((own, jnp.concatenate([text, before], axis=0)))
+    gathered = doubled(own, "blk", bits[:1])
+    gathered, logit_scale, logit_bias = lax.optimization_barrier((gathered, logit_scale, logit_bias))
+    gathered = doubled(doubled(gathered, "blk", bits[1:]), "sub", [1])
+    texts = doubled(both, "blk", bits)
+    scale, bias = logit_scale.reshape(1), logit_bias.reshape(1)
     block = (count, width)
-    after, peer, text_part, audio_part = pl.pallas_call(
-        functools.partial(logits_kernel, bits),
-        out_shape=[jax.ShapeDtypeStruct(block, t) for t in (BF16, BF16, F32, F32)],
-        in_specs=[SMEM, SMEM, SMEM, VMEM, VMEM, VMEM],
-        out_specs=[VMEM] * 4,
-        compiler_params=PARAMS,
-        name="logits",
-    )(place, logit_scale.reshape(1), logit_bias.reshape(1), gathered, proj_w, texts)
+    after, text_part, pair = pl.pallas_call(
+        text_kernel,
+        out_shape=[
+            jax.ShapeDtypeStruct(block, BF16),
+            jax.ShapeDtypeStruct(block, F32),
+            jax.ShapeDtypeStruct((2 * count, width), BF16),
+        ],
+        in_specs=[SMEM, SMEM, VMEM, VMEM, VMEM],
+        out_specs=[VMEM] * 3,
+        compiler_params=PARAMS,
+        name="text_side",
+    )(scale, bias, gathered, proj_w, both)
     after = passed_along(after, "grp", -1)
+    peer, audio_part = pl.pallas_call(
+        functools.partial(audio_kernel, bits),
+        out_shape=[jax.ShapeDtypeStruct(block, t) for t in (BF16, F32)],
+        in_specs=[SMEM, SMEM, VMEM, VMEM, VMEM],
+        out_specs=[VMEM] * 2,
+        compiler_params=PARAMS,
+        name="audio_side",
+    )(scale, bias, pair, gathered, texts)
     peer = swapped(peer, "sub", 1)
     return pl.pallas_call(
         sum_kernel,

time: 34.7 us -> 28.6 us (0.82); the launches traced: 34.1 us -> 28.4 us
  local copies, waits for them, and re-layouts: 4.97 us -> 0.03 us
  starting transfers between devices: 13.1 us -> 10.1 us
  waiting for transfers between devices: 7.9 us -> 9.71 us
  Pallas kernels: 6 us -> 6.57 us
    unnamed x14 -> x4, local copies, waits for them, and re-layouts: 4.97 us -> 0.02 us
    ppermute x6, starting transfers between devices: 13.1 us -> 9.51 us  [swapped(): return lax.ppermute(block, axis, [(i, i ^ bit) for i in devices])]
    ppermute x6, waiting for transfers between devices: 7.9 us -> 9.7 us  [swapped(): return lax.ppermute(block, axis, [(i, i ^ bit) for i in devices])]
    pallas_call x2 -> x3, Pallas kernels: 5.33 us -> 5.91 us  [the longest x1 4.43 us: on_device(): pl.pallas_call(tower_kernel, out_shape=[jax.ShapeDtypeStruct((count, chan...]
    ppermute x2, starting transfers between devices: 0.01 us -> 0.56 us  [passed_along(): lax.ppermute(block, axis, [((i - distance) % len(devices), i) for i in de...]
  transfers between devices with their start and end apart: 8 -> 8, of which waited for: 5 -> 5; matrix products, arithmetic and copies ran while one was open for 0% -> 0% of each run, Pallas kernels for 0% -> 21%
where the time goes in v2:
time: 28.6 us; the launch traced here: 28.4 us
  starting transfers between devices  10.1 us (35%)
  waiting for transfers between devices  9.71 us (34%)
  Pallas kernels  6.57 us (23%)
  between operations  2.02 us (7%)
    ppermute x6, waiting for transfers between devices, swapped(): return lax.ppermute(block, axis, [(i, i ^ bit) for i in devices])  9.7 us
    ppermute x6, starting transfers between devices, swapped(): return lax.ppermute(block, axis, [(i, i ^ bit) for i in devices])  9.51 us
    pallas_call x1, Pallas kernels, on_device(): pl.pallas_call(tower_kernel, out_shape=[jax.ShapeDtypeStruct((count, chan...  4.43 us
    pallas_call x1, Pallas kernels, on_device(): pl.pallas_call(text_kernel, out_shape=[jax.ShapeDtypeStruct(block, BF16),...  0.97 us
    pallas_call x1, Pallas kernels, on_device(): pl.pallas_call(sum_kernel, out_shape=[jax.ShapeDtypeStruct(block, F32)] *...  0.66 us
  transfers between devices with their start and end apart: 8, of which 5 were waited for; matrix products, arithmetic and copies ran while one was open for 0% of the time, Pallas kernels for 21%

profile of v2, /device:TPU:0, one launch (start us, length us, event | category | flops | bytes accessed | tf_op | source)
XLA Modules:
  0.0 28.4 jit_solution(4264550988189556413)
XLA Ops:
  0.6 0.0 copy-start
  0.6 0.5 %collective-permute-start = (bf16[16,1024]{1,0:T(8,128)(2,1)}, bf16[16,1024]{1,0:T(8,128)(2,1)S(1)}, u32[]{:S(2)}, u32[]{:S(2)}) collective-permute-start(bf16[16,1024]{1,0:T(8,128)(2,1)} %param.12), channel_id=1, source_target_pairs={{24,0},{0,8},{8,16},{16,24},{25,1},{1,9},{9,17},{17,25},{26,2},{2,... | collective-permute-start | bytes 98312 | tf_op jit(solution)/shard_map/ppermute | solution.py:26
  1.1 4.4 %tower.1 = (bf16[16,640]{1,0:T(8,128)(2,1)S(1)}, bf16[512,1024]{1,0:T(8,128)(2,1)S(1)}) custom-call(s32[16]{0:T(128)} %lengths_in.1, bf16[16,128,512]{2,1,0:T(8,128)(2,1)} %clips_in.1, s32[1,16]{1,0:T(1,128)} %assign_in.1, s32[1,16]{1,0:T(1,128)} %positives_in.1, bf16[1536,512]{1,0:T(8,128)(2,1)} %conv_in.1, bf16[512,1024]{1,0:T(8,128)(2,1)} %proj_in.1), custom_call_target="tpu_custom_call" | custom-call | flops 1610612736 | bytes 4194304 | tf_op jit(solution)/shard_map/tower/pallas_call | solution.py:195
  5.6 0.0 collective-permute-done
  5.6 0.0 copy-done
  5.6 3.7 %collective-permute-start.1 = (bf16[16,640]{1,0:T(8,128)(2,1)S(1)}, bf16[16,640]{1,0:T(8,128)(2,1)S(1)}, u32[]{:S(2)}, u32[]{:S(2)}) collective-permute-start(bf16[16,640]{1,0:T(8,128)(2,1)S(1)} %get-tuple-element.15), channel_id=1, source_target_pairs={{0,4},{2,6},{4,0},{6,2},{1,5},{3,7},{5,1},{7,3},{8,12},{10,14},{12... | collective-permute-start | bytes 61448 | tf_op jit(solution)/shard_map/ppermute | solution.py:21
  10.6 0.1 collective-permute-start.4
  10.7 0.4 %collective-permute-done.1 = bf16[16,640]{1,0:T(8,128)(2,1)S(1)} collective-permute-done((bf16[16,640]{1,0:T(8,128)(2,1)S(1)}, bf16[16,640]{1,0:T(8,128)(2,1)S(1)}, u32[]{:S(2)}, u32[]{:S(2)}) %collective-permute-start.1) | collective-permute-done | bytes 20512 | tf_op jit(solution)/shard_map/ppermute | solution.py:21
  11.0 1.9 %collective-permute-start.2 = (bf16[32,640]{1,0:T(8,128)(2,1)S(1)}, bf16[32,640]{1,0:T(8,128)(2,1)S(1)}, u32[]{:S(2)}, u32[]{:S(2)}) collective-permute-start(bf16[32,640]{1,0:T(8,128)(2,1)S(1)} %pad_maximum_fusion.4), channel_id=1, source_target_pairs={{0,2},{2,0},{4,6},{6,4},{1,3},{3,1},{5,7},{7,5},{8,10},{10,8},{12,... | collective-permute-start | bytes 122888 | tf_op jit(solution)/shard_map/ppermute | solution.py:21
  13.0 3.5 %collective-permute-done.2 = bf16[32,640]{1,0:T(8,128)(2,1)S(1)} collective-permute-done((bf16[32,640]{1,0:T(8,128)(2,1)S(1)}, bf16[32,640]{1,0:T(8,128)(2,1)S(1)}, u32[]{:S(2)}, u32[]{:S(2)}) %collective-permute-start.2) | collective-permute-done | bytes 40992 | tf_op jit(solution)/shard_map/ppermute | solution.py:21
  16.5 1.7 %collective-permute-start.3 = (bf16[64,640]{1,0:T(8,128)(2,1)S(1)}, bf16[64,640]{1,0:T(8,128)(2,1)S(1)}, u32[]{:S(2)}, u32[]{:S(2)}) collective-permute-start(bf16[64,640]{1,0:T(8,128)(2,1)S(1)} %pad_maximum_fusion.2), channel_id=1, source_target_pairs={{0,1},{1,0},{2,3},{3,2},{4,5},{5,4},{6,7},{7,6},{8,9},{9,8},{10,11... | collective-permute-start | bytes 245768 | tf_op jit(solution)/shard_map/ppermute | solution.py:21
  18.2 0.0 collective-permute-done.4
  18.2 0.6 %collective-permute-start.5 = (bf16[64,1024]{1,0:T(8,128)(2,1)S(1)}, bf16[64,1024]{1,0:T(8,128)(2,1)S(1)}, u32[]{:S(2)}, u32[]{:S(2)}) collective-permute-start(bf16[64,1024]{1,0:T(8,128)(2,1)S(1)} %pad_maximum_fusion.1), channel_id=1, source_target_pairs={{0,2},{2,0},{4,6},{6,4},{1,3},{3,1},{5,7},{7,5},{8,10},{10,8},{12,... | collective-permute-start | bytes 393224 | tf_op jit(solution)/shard_map/ppermute | solution.py:21
  18.8 2.2 %collective-permute-done.3 = bf16[64,640]{1,0:T(8,128)(2,1)S(1)} collective-permute-done((bf16[64,640]{1,0:T(8,128)(2,1)S(1)}, bf16[64,640]{1,0:T(8,128)(2,1)S(1)}, u32[]{:S(2)}, u32[]{:S(2)}) %collective-permute-start.3) | collective-permute-done | bytes 81952 | tf_op jit(solution)/shard_map/ppermute | solution.py:21
  21.0 1.0 %text_side.1 = (bf16[16,1024]{1,0:T(8,128)(2,1)S(1)}, f32[16,1024]{1,0:T(8,128)S(1)}, bf16[32,1024]{1,0:T(8,128)(2,1)S(1)}) custom-call(f32[1]{0:T(128)} %bitcast.2.scale, f32[1]{0:T(128)} %bitcast.4.bias, bf16[128,640]{1,0:T(8,128)(2,1)S(1)} %constant_dynamic-update-slice_fusion.gathered, bf16[512,1024]{1,0:T(8,128)(2,1)S(1)} %get-tuple-element.19.proj_w, ...), custom_call_target="tpu_custom_call" | custom-call | tf_op jit(solution)/shard_map/text_side/pallas_call | solution.py:228
  22.0 0.1 collective-permute-start.7
  22.1 1.2 %collective-permute-done.5 = bf16[64,1024]{1,0:T(8,128)(2,1)S(1)} collective-permute-done((bf16[64,1024]{1,0:T(8,128)(2,1)S(1)}, bf16[64,1024]{1,0:T(8,128)(2,1)S(1)}, u32[]{:S(2)}, u32[]{:S(2)}) %collective-permute-start.5) | collective-permute-done | bytes 131104 | tf_op jit(solution)/shard_map/ppermute | solution.py:21
  23.3 0.5 %audio_side.1 = (bf16[16,1024]{1,0:T(8,128)(2,1)S(1)}, f32[16,1024]{1,0:T(8,128)S(1)}) custom-call(f32[1]{0:T(128)} %bitcast.3.scale, f32[1]{0:T(128)} %bitcast.5.bias, bf16[32,1024]{1,0:T(8,128)(2,1)S(1)} %get-tuple-element.21.pair, bf16[128,640]{1,0:T(8,128)(2,1)S(1)} %constant_dynamic-update-slice_fusion.gathered, bf16[128,1024]{1,0:T(8,128)(2,1)S(1)} %pad_maximum_fusion.texts), custom_call_target="tpu_custom_call" | custom-call | tf_op jit(solution)/shard_map/audio_side/pallas_call | solution.py:241
  23.8 1.6 %collective-permute-start.6 = (bf16[16,1024]{1,0:T(8,128)(2,1)S(1)}, bf16[16,1024]{1,0:T(8,128)(2,1)S(1)}, u32[]{:S(2)}, u32[]{:S(2)}) collective-permute-start(bf16[16,1024]{1,0:T(8,128)(2,1)S(1)} %get-tuple-element.23), channel_id=1, source_target_pairs={{0,1},{1,0},{2,3},{3,2},{4,5},{5,4},{6,7},{7,6},{8,9},{9,8},{10,11... | collective-permute-start | bytes 98312 | tf_op jit(solution)/shard_map/ppermute | solution.py:21
  25.4 0.0 collective-permute-done.7.after
  25.4 2.4 %collective-permute-done.6.peer = bf16[16,1024]{1,0:T(8,128)(2,1)S(1)} collective-permute-done((bf16[16,1024]{1,0:T(8,128)(2,1)S(1)}, bf16[16,1024]{1,0:T(8,128)(2,1)S(1)}, u32[]{:S(2)}, u32[]{:S(2)}) %collective-permute-start.6) | collective-permute-done | bytes 32800 | tf_op jit(solution)/shard_map/ppermute | solution.py:21
  27.8 0.7 %sums.1 = (f32[16,1024]{1,0:T(8,128)}, f32[16,1024]{1,0:T(8,128)}) custom-call(f32[16,1024]{1,0:T(8,128)S(1)} %get-tuple-element.22.audio, bf16[16,1024]{1,0:T(8,128)(2,1)S(1)} %collective-permute-done.6.peer, f32[16,1024]{1,0:T(8,128)S(1)} %get-tuple-element.24.text, bf16[16,1024]{1,0:T(8,128)(2,1)S(1)} %collective-permute-done.7.after), custom_call_target="tpu_custom_call" | custom-call | tf_op jit(solution)/shard_map/sums/pallas_call | solution.py:250
  (8 shorter events, 0.1 us)
Async XLA Ops:
  0.6 5.0 %copy-start = (bf16[16,1024]{1,0:T(8,128)(2,1)S(1)}, bf16[16,1024]{1,0:T(8,128)(2,1)}, u32[]{:S(2)}) copy-start(bf16[16,1024]{1,0:T(8,128)(2,1)} %param.12) | copy-start | bytes 98308
  0.6 4.9 %collective-permute-start = (bf16[16,1024]{1,0:T(8,128)(2,1)}, bf16[16,1024]{1,0:T(8,128)(2,1)S(1)}, u32[]{:S(2)}, u32[]{:S(2)}) collective-permute-start(bf16[16,1024]{1,0:T(8,128)(2,1)} %param.12), channel_id=1, source_target_pairs={{24,0},{0,8},{8,16},{16,24},{25,1},{1,9},{9,17},{17,25},{26,2},{2,... | collective-permute-start | bytes 98312 | tf_op jit(solution)/shard_map/ppermute | solution.py:26
  5.6 5.4 %collective-permute-start.1 = (bf16[16,640]{1,0:T(8,128)(2,1)S(1)}, bf16[16,640]{1,0:T(8,128)(2,1)S(1)}, u32[]{:S(2)}, u32[]{:S(2)}) collective-permute-start(bf16[16,640]{1,0:T(8,128)(2,1)S(1)} %get-tuple-element.15), channel_id=1, source_target_pairs={{0,4},{2,6},{4,0},{6,2},{1,5},{3,7},{5,1},{7,3},{8,12},{10,14},{12... | collective-permute-start | bytes 61448 | tf_op jit(solution)/shard_map/ppermute | solution.py:21
  10.6 7.6 %collective-permute-start.4 = (bf16[32,1024]{1,0:T(8,128)(2,1)S(1)}, bf16[32,1024]{1,0:T(8,128)(2,1)S(1)}, u32[]{:S(2)}, u32[]{:S(2)}) collective-permute-start(bf16[32,1024]{1,0:T(8,128)(2,1)S(1)} %pad_maximum_fusion.3.texts), channel_id=1, source_target_pairs={{0,4},{2,6},{4,0},{6,2},{1,5},{3,7},{5,1},{7,3},{8,12},{10,14},{12... | collective-permute-start | bytes 196616 | tf_op jit(solution)/shard_map/ppermute | solution.py:21
  11.0 5.4 %collective-permute-start.2 = (bf16[32,640]{1,0:T(8,128)(2,1)S(1)}, bf16[32,640]{1,0:T(8,128)(2,1)S(1)}, u32[]{:S(2)}, u32[]{:S(2)}) collective-permute-start(bf16[32,640]{1,0:T(8,128)(2,1)S(1)} %pad_maximum_fusion.4), channel_id=1, source_target_pairs={{0,2},{2,0},{4,6},{6,4},{1,3},{3,1},{5,7},{7,5},{8,10},{10,8},{12,... | collective-permute-start | bytes 122888 | tf_op jit(solution)/shard_map/ppermute | solution.py:21
  16.5 4.5 %collective-permute-start.3 = (bf16[64,640]{1,0:T(8,128)(2,1)S(1)}, bf16[64,640]{1,0:T(8,128)(2,1)S(1)}, u32[]{:S(2)}, u32[]{:S(2)}) collective-permute-start(bf16[64,640]{1,0:T(8,128)(2,1)S(1)} %pad_maximum_fusion.2), channel_id=1, source_target_pairs={{0,1},{1,0},{2,3},{3,2},{4,5},{5,4},{6,7},{7,6},{8,9},{9,8},{10,11... | collective-permute-start | bytes 245768 | tf_op jit(solution)/shard_map/ppermute | solution.py:21
  18.2 5.0 %collective-permute-start.5 = (bf16[64,1024]{1,0:T(8,128)(2,1)S(1)}, bf16[64,1024]{1,0:T(8,128)(2,1)S(1)}, u32[]{:S(2)}, u32[]{:S(2)}) collective-permute-start(bf16[64,1024]{1,0:T(8,128)(2,1)S(1)} %pad_maximum_fusion.1), channel_id=1, source_target_pairs={{0,2},{2,0},{4,6},{6,4},{1,3},{3,1},{5,7},{7,5},{8,10},{10,8},{12,... | collective-permute-start | bytes 393224 | tf_op jit(solution)/shard_map/ppermute | solution.py:21
  22.0 3.4 %collective-permute-start.7 = (bf16[16,1024]{1,0:T(8,128)(2,1)S(1)}, bf16[16,1024]{1,0:T(8,128)(2,1)S(1)}, u32[]{:S(2)}, u32[]{:S(2)}) collective-permute-start(bf16[16,1024]{1,0:T(8,128)(2,1)S(1)} %get-tuple-element.25), channel_id=1, source_target_pairs={{8,0},{16,8},{24,16},{0,24},{9,1},{17,9},{25,17},{1,25},{10,2},{18... | collective-permute-start | bytes 98312 | tf_op jit(solution)/shard_map/ppermute | solution.py:26
  23.8 4.0 %collective-permute-start.6 = (bf16[16,1024]{1,0:T(8,128)(2,1)S(1)}, bf16[16,1024]{1,0:T(8,128)(2,1)S(1)}, u32[]{:S(2)}, u32[]{:S(2)}) collective-permute-start(bf16[16,1024]{1,0:T(8,128)(2,1)S(1)} %get-tuple-element.23), channel_id=1, source_target_pairs={{0,1},{1,0},{2,3},{3,2},{4,5},{5,4},{6,7},{7,6},{8,9},{9,8},{10,11... | collective-permute-start | bytes 98312 | tf_op jit(solution)/shard_map/ppermute | solution.py:21

commit v3 on v2

--- a/solution.py
+++ b/solution.py
@@ -1,4 +1,5 @@
 import functools
+import math
 
 import jax
 import jax.numpy as jnp
@@ -21,6 +22,18 @@
     return lax.ppermute(block, axis, [(i, i ^ bit) for i in devices])
 
 
+def swapped_over(block, axes, bits):
+    sizes = [lax.axis_size(axis) for axis in axes]
+    route = []
+    for i in range(math.prod(sizes)):
+        rest, away, stride = i, 0, 1
+        for size, bit in zip(reversed(sizes), reversed(bits)):
+            away += (rest % size ^ bit) * stride
+            rest, stride = rest // size, stride * size
+        route.append((i, away))
+    return lax.ppermute(block, axes, route)
+
+
 def passed_along(block, axis, distance):
     devices = range(lax.axis_size(axis))
     return lax.ppermute(block, axis, [((i - distance) % len(devices), i) for i in devices])
@@ -46,13 +59,6 @@
     at = lax.broadcasted_iota(jnp.int32, (size, size), 0)
     lane = lax.broadcasted_iota(jnp.int32, (size, size), 1)
     return jnp.sum(jnp.where(at == lane, jnp.broadcast_to(row, (size, size)), 0.0), 1, keepdims=True)
-
-
-def as_row(column):
-    size = column.shape[0]
-    at = lax.broadcasted_iota(jnp.int32, (size, size), 0)
-    lane = lax.broadcasted_iota(jnp.int32, (size, size), 1)
-    return jnp.sum(jnp.where(at == lane, jnp.broadcast_to(column, (size, size)), 0.0), 0, keepdims=True)
 
 
 def product(a, b, b_axis=0):
@@ -74,7 +80,7 @@
     copies.append(pltpu.make_async_copy(assign_in, assign, sems.at[6]))
     copies.append(pltpu.make_async_copy(positives_in, positives, sems.at[7]))
     copies.append(pltpu.make_async_copy(proj_in, proj_w, sems.at[8]))
-    for copy in copies:
+    for copy in copies[:-1]:
         copy.start()
     wide[:, :, 0:8, :] = jnp.zeros((wide.shape[0], channels // LANES, 8, LANES), F32)
     rows = lax.broadcasted_iota(jnp.int32, (half, 1), 0)
@@ -97,16 +103,20 @@
             for tap, values in enumerate(taps):
                 first = tap * channels + k * LANES
                 stacked[base : base + half, first : first + LANES] = values.astype(BF16)
+    copies[-1].start()
     for copy in copies[5:-1]:
         copy.wait()
-    hidden = gelu(product(stacked[...], conv_w[...]))
     pooled = []
-    for c in range(count):
-        valid = 2 * rows < lengths[c]
-        total = jnp.sum(
-            jnp.where(valid, hidden[c * half : (c + 1) * half], 0.0), axis=0, keepdims=True
-        )
-        pooled.append(total / ((lengths[c] + 1) // 2).astype(F32))
+    step = parts * half
+    for n in range(4):
+        hidden = gelu(product(stacked[n * step : (n + 1) * step], conv_w[...]))
+        for c in range(parts):
+            length = lengths[n * parts + c]
+            valid = 2 * rows < length
+            total = jnp.sum(
+                jnp.where(valid, hidden[c * half : (c + 1) * half], 0.0), axis=0, keepdims=True
+            )
+            pooled.append(total / ((length + 1) // 2).astype(F32))
     out[:, 0:channels] = jnp.concatenate(pooled, axis=0).astype(BF16)
     slots = as_column(assign[...].astype(F32))
     low = as_column((positives[...] & 255).astype(F32))
@@ -125,13 +135,21 @@
     return jnp.where(hit, -jax.nn.sigmoid(-logits), jax.nn.sigmoid(logits)).astype(BF16)
 
 
-def text_kernel(scale, bias, gathered, proj_w, texts, after_out, text_out, pair_out):
-    channels = proj_w.shape[0]
+def next_kernel(scale, bias, gathered, proj_w, texts, after_out, audio_out):
+    count = after_out.shape[0]
+    audio = normalized(product(gathered[:, 0 : proj_w.shape[0]], proj_w[...]))
+    audio_out[...] = audio
+    zt = normalized(texts[count:].astype(F32))
+    logits = scale[0] * product(zt, audio, 1) + bias[0]
+    after_out[...] = (scale[0] * product(jax.nn.sigmoid(logits).astype(BF16), audio)).astype(BF16)
+
+
+def own_kernel(scale, bias, gathered, audio, texts, text_out, pair_out):
     rows = gathered.shape[0]
     count = text_out.shape[0]
+    channels = gathered.shape[1] - LANES
     column = rows // 2
     blk, sub = lax.axis_index("blk"), lax.axis_index("sub")
-    scale, bias = scale[0], bias[0]
     marks = gathered[:, channels : channels + LANES].astype(F32)
     slot = marks[:, 0:1].astype(jnp.int32)
     match = marks[:, 1:2] + 256.0 * marks[:, 2:3]
@@ -139,18 +157,14 @@
     block = here % column // count
     source = (slot // count ^ sub) * column + block * count + slot % count
     lane = lax.broadcasted_iota(jnp.int32, (rows, rows), 1)
-    pick = jnp.where(lane == source, 1.0, 0.0).astype(BF16)
-    pooled = product(pick, gathered[:, 0:channels]).astype(BF16)
-    audio = normalized(product(pooled, proj_w[...]))
-    pair_out[0:count] = audio[0:count]
-    pair_out[count:] = audio[column : column + count]
-    zt = normalized(texts[0 : 2 * count].astype(F32))
-    logits = scale * product(zt, audio, 1) + bias
-    at = lax.broadcasted_iota(jnp.int32, (2 * count, 1), 0)
-    wanted = jnp.where(at < count, (blk * 2 + sub) * count + at, -1).astype(F32)
-    pulled = scale * product(weights(logits, wanted == as_row(match)), audio)
-    after_out[...] = pulled[count:].astype(BF16)
-    text_out[...] = pulled[:count]
+    picked = lane == source
+    near = jnp.concatenate([picked[0:count], picked[column : column + count]], axis=0)
+    pair_out[...] = product(jnp.where(near, 1.0, 0.0).astype(BF16), audio[...]).astype(BF16)
+    wanted_by = jnp.sum(jnp.where(picked, jnp.broadcast_to(match, (rows, rows)), 0.0), 0, keepdims=True)
+    zt = normalized(texts[0:count].astype(F32))
+    logits = scale[0] * product(zt, audio[...], 1) + bias[0]
+    at = lax.broadcasted_iota(jnp.int32, (count, 1), 0) + (blk * 2 + sub) * count
+    text_out[...] = scale[0] * product(weights(logits, at.astype(F32) == wanted_by), audio[...])
 
 
 def audio_kernel(bits, scale, bias, pair, gathered, texts, peer_out, audio_out):
@@ -185,14 +199,10 @@
     return pltpu.with_memory_space_constraint(array, pltpu.HBM)
 
 
-def on_device(clips, lengths, assign, text, positives, conv_w, proj_w, logit_scale, logit_bias):
+def tower(clips, lengths, assign, positives, conv_w, proj_w):
     count, frames, channels = clips.shape
-    width = text.shape[1]
-    assert lax.axis_size("sub") == 2 and count <= 128 and count % 4 == 0
-    bits = bits_of(lax.axis_size("blk"))
-    before = passed_along(text, "grp", 1)
     inputs = (lengths, clips, assign, positives, conv_w, proj_w)
-    own, proj_w = pl.pallas_call(
+    return pl.pallas_call(
         tower_kernel,
         out_shape=[
             jax.ShapeDtypeStruct((count, channels + LANES), BF16),
@@ -218,25 +228,60 @@
         ),
         name="tower",
     )(*map(in_hbm, inputs))
+
+
+def on_device(clips, lengths, assign, text, positives, conv_w, proj_w, logit_scale, logit_bias):
+    count, frames, channels = clips.shape
+    width = text.shape[1]
+    assert lax.axis_size("sub") == 2 and count <= 128 and count % 4 == 0
+    bits = bits_of(lax.axis_size("blk"))
+    before = passed_along(text, "grp", 1)
+    own, proj_w = tower(clips, lengths, assign, positives, conv_w, proj_w)
     own, both = lax.optimization_barrier((own, jnp.concatenate([text, before], axis=0)))
-    gathered = doubled(own, "blk", bits[:1])
-    gathered, logit_scale, logit_bias = lax.optimization_barrier((gathered, logit_scale, logit_bias))
-    gathered = doubled(doubled(gathered, "blk", bits[1:]), "sub", [1])
-    texts = doubled(both, "blk", bits)
+    gathered = doubled(own, "blk", bits[:-1])
+    gathered, logit_scale, logit_bias = lax.optimization_barrier(
+        (gathered, logit_scale, logit_bias)
+    )
+    last = bits[-1:]
+    gathered = jnp.concatenate(
+        [
+            gathered,
+            swapped_over(gathered, ("blk",), last),
+            swapped_over(gathered, ("sub",), [1]),
+            swapped_over(gathered, ("blk", "sub"), last + [1]),
+        ],
+        axis=0,
+    )
+    texts = doubled(both, "blk", bits[:-1])
+    beside = swapped(both, "blk", bits[-1])
+    texts, beside = lax.optimization_barrier((texts, beside))
+    texts = jnp.concatenate(
+        [texts, beside, swapped(texts[2 * count :], "blk", bits[-1])], axis=0
+    )
     scale, bias = logit_scale.reshape(1), logit_bias.reshape(1)
     block = (count, width)
-    after, text_part, pair = pl.pallas_call(
-        text_kernel,
+    after, audio = pl.pallas_call(
+        next_kernel,
         out_shape=[
             jax.ShapeDtypeStruct(block, BF16),
+            jax.ShapeDtypeStruct((gathered.shape[0], width), BF16),
+        ],
+        in_specs=[SMEM, SMEM, VMEM, VMEM, VMEM],
+        out_specs=[VMEM] * 2,
+        compiler_params=PARAMS,
+        name="next_texts",
+    )(scale, bias, gathered, proj_w, both)
+    text_part, pair = pl.pallas_call(
+        own_kernel,
+        out_shape=[
             jax.ShapeDtypeStruct(block, F32),
             jax.ShapeDtypeStruct((2 * count, width), BF16),
         ],
         in_specs=[SMEM, SMEM, VMEM, VMEM, VMEM],
-        out_specs=[VMEM] * 3,
-        compiler_params=PARAMS,
-        name="text_side",
-    )(scale, bias, gathered, proj_w, both)
+        out_specs=[VMEM] * 2,
+        compiler_params=PARAMS,
+        name="own_texts",
+    )(scale, bias, gathered, audio, both)
     after = passed_along(after, "grp", -1)
     peer, audio_part = pl.pallas_call(
         functools.partial(audio_kernel, bits),

time: 28.6 us -> 27.3 us (0.955)
  waiting for transfers between devices: 9.71 us -> 5.03 us
  starting transfers between devices: 10.1 us -> 13.2 us
    ppermute x6 -> x5, waiting for transfers between devices: 9.7 us -> 2.62 us  [swapped(): return lax.ppermute(block, axis, [(i, i ^ bit) for i in devices])]
    ppermute x0 -> x3, starting transfers between devices: none -> 3.55 us  [swapped_over(): return lax.ppermute(block, axes, route)]
    ppermute x0 -> x3, waiting for transfers between devices: none -> 2.41 us  [swapped_over(): return lax.ppermute(block, axes, route)]
    ppermute x6 -> x5, starting transfers between devices: 9.51 us -> 9.15 us  [swapped(): return lax.ppermute(block, axis, [(i, i ^ bit) for i in devices])]
    pallas_call x2 -> x3, Pallas kernels: 5.4 us -> 5.53 us  [the longest x1 4.25 us: tower(): pl.pallas_call(tower_kernel, out_shape=[jax.ShapeDtypeStruct((count, chan...]
  transfers between devices with their start and end apart: 8 -> 10, of which waited for: 5 -> 5; matrix products, arithmetic and copies ran while one was open for 0% -> 0% of each run, Pallas kernels for 21% -> 22%
where the time goes in v3:
time: 27.3 us; the launch traced here: 27.1 us
  starting transfers between devices  13.2 us (48%)
  Pallas kernels  6.7 us (25%)
  waiting for transfers between devices  5.03 us (18%)
  between operations  2.03 us (7%)
    ppermute x5, starting transfers between devices, swapped(): return lax.ppermute(block, axis, [(i, i ^ bit) for i in devices])  9.15 us
    pallas_call x1, Pallas kernels, tower(): pl.pallas_call(tower_kernel, out_shape=[jax.ShapeDtypeStruct((count, chan...  4.25 us
    ppermute x3, starting transfers between devices, swapped_over(): return lax.ppermute(block, axes, route)  3.55 us
    ppermute x5, waiting for transfers between devices, swapped(): return lax.ppermute(block, axis, [(i, i ^ bit) for i in devices])  2.62 us
    ppermute x3, waiting for transfers between devices, swapped_over(): return lax.ppermute(block, axes, route)  2.41 us
    pallas_call x1, Pallas kernels, on_device(): pl.pallas_call(next_kernel, out_shape=[jax.ShapeDtypeStruct(block, BF16),...  0.76 us
    pallas_call x1, Pallas kernels, on_device(): pl.pallas_call(sum_kernel, out_shape=[jax.ShapeDtypeStruct(block, F32)] *...  0.66 us
    ppermute x2, starting transfers between devices, passed_along(): lax.ppermute(block, axis, [((i - distance) % len(devices), i) for i in de...  0.55 us
  transfers between devices with their start and end apart: 10, of which 5 were waited for; matrix products, arithmetic and copies ran while one was open for 0% of the time, Pallas kernels for 22%

profile of v3, /device:TPU:0, one launch (start us, length us, event | category | flops | bytes accessed | tf_op | source)
XLA Modules:
  0.0 27.1 jit_solution(9322763182742945910)
XLA Ops:
  0.6 0.0 copy-start
  0.6 0.5 %collective-permute-start = (bf16[16,1024]{1,0:T(8,128)(2,1)}, bf16[16,1024]{1,0:T(8,128)(2,1)S(1)}, u32[]{:S(2)}, u32[]{:S(2)}) collective-permute-start(bf16[16,1024]{1,0:T(8,128)(2,1)} %param.12), channel_id=1, source_target_pairs={{24,0},{0,8},{8,16},{16,24},{25,1},{1,9},{9,17},{17,25},{26,2},{2,... | collective-permute-start | bytes 98312 | tf_op jit(solution)/shard_map/ppermute | solution.py:39
  1.1 4.2 %tower.1 = (bf16[16,640]{1,0:T(8,128)(2,1)S(1)}, bf16[512,1024]{1,0:T(8,128)(2,1)S(1)}) custom-call(s32[16]{0:T(128)} %lengths_in.1, bf16[16,128,512]{2,1,0:T(8,128)(2,1)} %clips_in.1, s32[1,16]{1,0:T(1,128)} %assign_in.1, s32[1,16]{1,0:T(1,128)} %positives_in.1, bf16[1536,512]{1,0:T(8,128)(2,1)} %conv_in.1, bf16[512,1024]{1,0:T(8,128)(2,1)} %proj_in.1), custom_call_target="tpu_custom_call" | custom-call | flops 1610612736 | bytes 4194304 | tf_op jit(solution)/shard_map/tower/pallas_call | solution.py:205
  5.4 0.0 collective-permute-done
  5.4 0.0 copy-done
  5.4 3.7 %collective-permute-start.1 = (bf16[16,640]{1,0:T(8,128)(2,1)S(1)}, bf16[16,640]{1,0:T(8,128)(2,1)S(1)}, u32[]{:S(2)}, u32[]{:S(2)}) collective-permute-start(bf16[16,640]{1,0:T(8,128)(2,1)S(1)} %get-tuple-element.18), channel_id=1, source_target_pairs={{0,4},{2,6},{4,0},{6,2},{1,5},{3,7},{5,1},{7,3},{8,12},{10,14},{12... | collective-permute-start | bytes 61448 | tf_op jit(solution)/shard_map/ppermute | solution.py:22
  10.4 0.1 collective-permute-start.5
  10.5 1.9 %collective-permute-start.6 = (bf16[32,1024]{1,0:T(8,128)(2,1)S(1)}, bf16[32,1024]{1,0:T(8,128)(2,1)S(1)}, u32[]{:S(2)}, u32[]{:S(2)}) collective-permute-start(bf16[32,1024]{1,0:T(8,128)(2,1)S(1)} %pad_maximum_fusion.2.texts), channel_id=1, source_target_pairs={{0,2},{2,0},{4,6},{6,4},{1,3},{3,1},{5,7},{7,5},{8,10},{10,8},{12,... | collective-permute-start | bytes 196616 | tf_op jit(solution)/shard_map/ppermute | solution.py:22
  12.4 0.0 collective-permute-done.1
  12.4 0.4 %collective-permute-start.2 = (bf16[32,640]{1,0:T(8,128)(2,1)S(1)}, bf16[32,640]{1,0:T(8,128)(2,1)S(1)}, u32[]{:S(2)}, u32[]{:S(2)}) collective-permute-start(bf16[32,640]{1,0:T(8,128)(2,1)S(1)} %pad_maximum_fusion.3), channel_id=1, source_target_pairs={{0,2},{2,0},{4,6},{6,4},{1,3},{3,1},{5,7},{7,5},{8,10},{10,8},{12,... | collective-permute-start | bytes 122888 | tf_op jit(solution)/shard_map/ppermute | solution.py:34
  12.8 1.6 %collective-permute-start.3 = (bf16[32,640]{1,0:T(8,128)(2,1)S(1)}, bf16[32,640]{1,0:T(8,128)(2,1)S(1)}, u32[]{:S(2)}, u32[]{:S(2)}) collective-permute-start(bf16[32,640]{1,0:T(8,128)(2,1)S(1)} %pad_maximum_fusion.3), channel_id=1, source_target_pairs={{0,1},{1,0},{2,3},{3,2},{4,5},{5,4},{6,7},{7,6},{8,9},{9,8},{10,11... | collective-permute-start | bytes 122888 | tf_op jit(solution)/shard_map/ppermute | solution.py:34
  14.4 1.5 %collective-permute-start.4 = (bf16[32,640]{1,0:T(8,128)(2,1)S(1)}, bf16[32,640]{1,0:T(8,128)(2,1)S(1)}, u32[]{:S(2)}, u32[]{:S(2)}) collective-permute-start(bf16[32,640]{1,0:T(8,128)(2,1)S(1)} %pad_maximum_fusion.3), channel_id=1, source_target_pairs={{0,3},{1,2},{2,1},{3,0},{4,7},{5,6},{6,5},{7,4},{8,11},{9,10},{10,... | collective-permute-start | bytes 122888 | tf_op jit(solution)/shard_map/ppermute | solution.py:34
  15.9 1.2 %collective-permute-done.2 = bf16[32,640]{1,0:T(8,128)(2,1)S(1)} collective-permute-done((bf16[32,640]{1,0:T(8,128)(2,1)S(1)}, bf16[32,640]{1,0:T(8,128)(2,1)S(1)}, u32[]{:S(2)}, u32[]{:S(2)}) %collective-permute-start.2) | collective-permute-done | bytes 40992 | tf_op jit(solution)/shard_map/ppermute | solution.py:34
  17.1 0.0 collective-permute-done.3
  17.2 0.1 collective-permute-done.5
  17.3 0.0 collective-permute-done.6
  17.3 1.3 %collective-permute-start.7 = (bf16[32,1024]{1,0:T(8,128)(2,1)S(1)}, bf16[32,1024]{1,0:T(8,128)(2,1)S(1)}, u32[]{:S(2)}, u32[]{:S(2)}) collective-permute-start(bf16[32,1024]{1,0:T(8,128)(2,1)S(1)} %slice.3), channel_id=1, source_target_pairs={{0,2},{2,0},{4,6},{6,4},{1,3},{3,1},{5,7},{7,5},{8,10},{10,8},{12,... | collective-permute-start | bytes 196616 | tf_op jit(solution)/shard_map/ppermute | solution.py:22
  18.6 1.2 %collective-permute-done.4 = bf16[32,640]{1,0:T(8,128)(2,1)S(1)} collective-permute-done((bf16[32,640]{1,0:T(8,128)(2,1)S(1)}, bf16[32,640]{1,0:T(8,128)(2,1)S(1)}, u32[]{:S(2)}, u32[]{:S(2)}) %collective-permute-start.4) | collective-permute-done | bytes 40992 | tf_op jit(solution)/shard_map/ppermute | solution.py:34
  19.8 0.8 %next_texts.1 = (bf16[16,1024]{1,0:T(8,128)(2,1)S(1)}, bf16[128,1024]{1,0:T(8,128)(2,1)S(1)}) custom-call(f32[1]{0:T(128)} %bitcast.2.scale, f32[1]{0:T(128)} %bitcast.5.bias, bf16[128,640]{1,0:T(8,128)(2,1)S(1)} %constant_dynamic-update-slice_fusion.gathered, bf16[512,1024]{1,0:T(8,128)(2,1)S(1)} %get-tuple-element.22.proj_w, ...), custom_call_target="tpu_custom_call" | custom-call | tf_op jit(solution)/shard_map/next_texts/pallas_call | solution.py:263
  20.6 0.0 collective-permute-start.9
  20.7 0.5 %own_texts.1 = (f32[16,1024]{1,0:T(8,128)S(1)}, bf16[32,1024]{1,0:T(8,128)(2,1)S(1)}) custom-call(f32[1]{0:T(128)} %bitcast.3.scale, f32[1]{0:T(128)} %bitcast.6.bias, bf16[128,640]{1,0:T(8,128)(2,1)S(1)} %constant_dynamic-update-slice_fusion.gathered, bf16[128,1024]{1,0:T(8,128)(2,1)S(1)} %get-tuple-element.24.audio, ...), custom_call_target="tpu_custom_call" | custom-call | tf_op jit(solution)/shard_map/own_texts/pallas_call | solution.py:274
  21.2 0.6 %collective-permute-done.7 = bf16[32,1024]{1,0:T(8,128)(2,1)S(1)} collective-permute-done((bf16[32,1024]{1,0:T(8,128)(2,1)S(1)}, bf16[32,1024]{1,0:T(8,128)(2,1)S(1)}, u32[]{:S(2)}, u32[]{:S(2)}) %collective-permute-start.7) | collective-permute-done | bytes 65568 | tf_op jit(solution)/shard_map/ppermute | solution.py:22
  21.8 0.5 %audio_side.1 = (bf16[16,1024]{1,0:T(8,128)(2,1)S(1)}, f32[16,1024]{1,0:T(8,128)S(1)}) custom-call(f32[1]{0:T(128)} %bitcast.4.scale, f32[1]{0:T(128)} %bitcast.7.bias, bf16[32,1024]{1,0:T(8,128)(2,1)S(1)} %get-tuple-element.25.pair, bf16[128,640]{1,0:T(8,128)(2,1)S(1)} %constant_dynamic-update-slice_fusion.gathered, bf16[128,1024]{1,0:T(8,128)(2,1)S(1)} %pad_maximum_fusion.texts), custom_call_target="tpu_custom_call" | custom-call | tf_op jit(solution)/shard_map/audio_side/pallas_call | solution.py:286
  22.3 2.2 %collective-permute-start.8 = (bf16[16,1024]{1,0:T(8,128)(2,1)S(1)}, bf16[16,1024]{1,0:T(8,128)(2,1)S(1)}, u32[]{:S(2)}, u32[]{:S(2)}) collective-permute-start(bf16[16,1024]{1,0:T(8,128)(2,1)S(1)} %get-tuple-element.29), channel_id=1, source_target_pairs={{0,1},{1,0},{2,3},{3,2},{4,5},{5,4},{6,7},{7,6},{8,9},{9,8},{10,11... | collective-permute-start | bytes 98312 | tf_op jit(solution)/shard_map/ppermute | solution.py:22
  24.5 0.0 collective-permute-done.9.after
  24.5 1.9 %collective-permute-done.8.peer = bf16[16,1024]{1,0:T(8,128)(2,1)S(1)} collective-permute-done((bf16[16,1024]{1,0:T(8,128)(2,1)S(1)}, bf16[16,1024]{1,0:T(8,128)(2,1)S(1)}, u32[]{:S(2)}, u32[]{:S(2)}) %collective-permute-start.8) | collective-permute-done | bytes 32800 | tf_op jit(solution)/shard_map/ppermute | solution.py:22
  26.4 0.7 %sums.1 = (f32[16,1024]{1,0:T(8,128)}, f32[16,1024]{1,0:T(8,128)}) custom-call(f32[16,1024]{1,0:T(8,128)S(1)} %get-tuple-element.28.audio, bf16[16,1024]{1,0:T(8,128)(2,1)S(1)} %collective-permute-done.8.peer, f32[16,1024]{1,0:T(8,128)S(1)} %get-tuple-element.30.text, bf16[16,1024]{1,0:T(8,128)(2,1)S(1)} %collective-permute-done.9.after), custom_call_target="tpu_custom_call" | custom-call | tf_op jit(solution)/shard_map/sums/pallas_call | solution.py:295
  (9 shorter events, 0.1 us)
Async XLA Ops:
  0.6 4.8 %copy-start = (bf16[16,1024]{1,0:T(8,128)(2,1)S(1)}, bf16[16,1024]{1,0:T(8,128)(2,1)}, u32[]{:S(2)}) copy-start(bf16[16,1024]{1,0:T(8,128)(2,1)} %param.12) | copy-start | bytes 98308
  0.6 4.8 %collective-permute-start = (bf16[16,1024]{1,0:T(8,128)(2,1)}, bf16[16,1024]{1,0:T(8,128)(2,1)S(1)}, u32[]{:S(2)}, u32[]{:S(2)}) collective-permute-start(bf16[16,1024]{1,0:T(8,128)(2,1)} %param.12), channel_id=1, source_target_pairs={{24,0},{0,8},{8,16},{16,24},{25,1},{1,9},{9,17},{17,25},{26,2},{2,... | collective-permute-start | bytes 98312 | tf_op jit(solution)/shard_map/ppermute | solution.py:39
  5.4 7.0 %collective-permute-start.1 = (bf16[16,640]{1,0:T(8,128)(2,1)S(1)}, bf16[16,640]{1,0:T(8,128)(2,1)S(1)}, u32[]{:S(2)}, u32[]{:S(2)}) collective-permute-start(bf16[16,640]{1,0:T(8,128)(2,1)S(1)} %get-tuple-element.18), channel_id=1, source_target_pairs={{0,4},{2,6},{4,0},{6,2},{1,5},{3,7},{5,1},{7,3},{8,12},{10,14},{12... | collective-permute-start | bytes 61448 | tf_op jit(solution)/shard_map/ppermute | solution.py:22
  10.4 6.8 %collective-permute-start.5 = (bf16[32,1024]{1,0:T(8,128)(2,1)S(1)}, bf16[32,1024]{1,0:T(8,128)(2,1)S(1)}, u32[]{:S(2)}, u32[]{:S(2)}) collective-permute-start(bf16[32,1024]{1,0:T(8,128)(2,1)S(1)} %pad_maximum_fusion.2.texts), channel_id=1, source_target_pairs={{0,4},{2,6},{4,0},{6,2},{1,5},{3,7},{5,1},{7,3},{8,12},{10,14},{12... | collective-permute-start | bytes 196616 | tf_op jit(solution)/shard_map/ppermute | solution.py:22
  10.5 6.8 %collective-permute-start.6 = (bf16[32,1024]{1,0:T(8,128)(2,1)S(1)}, bf16[32,1024]{1,0:T(8,128)(2,1)S(1)}, u32[]{:S(2)}, u32[]{:S(2)}) collective-permute-start(bf16[32,1024]{1,0:T(8,128)(2,1)S(1)} %pad_maximum_fusion.2.texts), channel_id=1, source_target_pairs={{0,2},{2,0},{4,6},{6,4},{1,3},{3,1},{5,7},{7,5},{8,10},{10,8},{12,... | collective-permute-start | bytes 196616 | tf_op jit(solution)/shard_map/ppermute | solution.py:22
  12.4 4.7 %collective-permute-start.2 = (bf16[32,640]{1,0:T(8,128)(2,1)S(1)}, bf16[32,640]{1,0:T(8,128)(2,1)S(1)}, u32[]{:S(2)}, u32[]{:S(2)}) collective-permute-start(bf16[32,640]{1,0:T(8,128)(2,1)S(1)} %pad_maximum_fusion.3), channel_id=1, source_target_pairs={{0,2},{2,0},{4,6},{6,4},{1,3},{3,1},{5,7},{7,5},{8,10},{10,8},{12,... | collective-permute-start | bytes 122888 | tf_op jit(solution)/shard_map/ppermute | solution.py:34
  12.8 4.4 %collective-permute-start.3 = (bf16[32,640]{1,0:T(8,128)(2,1)S(1)}, bf16[32,640]{1,0:T(8,128)(2,1)S(1)}, u32[]{:S(2)}, u32[]{:S(2)}) collective-permute-start(bf16[32,640]{1,0:T(8,128)(2,1)S(1)} %pad_maximum_fusion.3), channel_id=1, source_target_pairs={{0,1},{1,0},{2,3},{3,2},{4,5},{5,4},{6,7},{7,6},{8,9},{9,8},{10,11... | collective-permute-start | bytes 122888 | tf_op jit(solution)/shard_map/ppermute | solution.py:34
  14.4 5.4 %collective-permute-start.4 = (bf16[32,640]{1,0:T(8,128)(2,1)S(1)}, bf16[32,640]{1,0:T(8,128)(2,1)S(1)}, u32[]{:S(2)}, u32[]{:S(2)}) collective-permute-start(bf16[32,640]{1,0:T(8,128)(2,1)S(1)} %pad_maximum_fusion.3), channel_id=1, source_target_pairs={{0,3},{1,2},{2,1},{3,0},{4,7},{5,6},{6,5},{7,4},{8,11},{9,10},{10,... | collective-permute-start | bytes 122888 | tf_op jit(solution)/shard_map/ppermute | solution.py:34
  17.3 4.5 %collective-permute-start.7 = (bf16[32,1024]{1,0:T(8,128)(2,1)S(1)}, bf16[32,1024]{1,0:T(8,128)(2,1)S(1)}, u32[]{:S(2)}, u32[]{:S(2)}) collective-permute-start(bf16[32,1024]{1,0:T(8,128)(2,1)S(1)} %slice.3), channel_id=1, source_target_pairs={{0,2},{2,0},{4,6},{6,4},{1,3},{3,1},{5,7},{7,5},{8,10},{10,8},{12,... | collective-permute-start | bytes 196616 | tf_op jit(solution)/shard_map/ppermute | solution.py:22
  20.6 3.9 %collective-permute-start.9 = (bf16[16,1024]{1,0:T(8,128)(2,1)S(1)}, bf16[16,1024]{1,0:T(8,128)(2,1)S(1)}, u32[]{:S(2)}, u32[]{:S(2)}) collective-permute-start(bf16[16,1024]{1,0:T(8,128)(2,1)S(1)} %get-tuple-element.31), channel_id=1, source_target_pairs={{8,0},{16,8},{24,16},{0,24},{9,1},{17,9},{25,17},{1,25},{10,2},{18... | collective-permute-start | bytes 98312 | tf_op jit(solution)/shard_map/ppermute | solution.py:39
  22.3 4.1 %collective-permute-start.8 = (bf16[16,1024]{1,0:T(8,128)(2,1)S(1)}, bf16[16,1024]{1,0:T(8,128)(2,1)S(1)}, u32[]{:S(2)}, u32[]{:S(2)}) collective-permute-start(bf16[16,1024]{1,0:T(8,128)(2,1)S(1)} %get-tuple-element.29), channel_id=1, source_target_pairs={{0,1},{1,0},{2,3},{3,2},{4,5},{5,4},{6,7},{7,6},{8,9},{9,8},{10,11... | collective-permute-start | bytes 98312 | tf_op jit(solution)/shard_map/ppermute | solution.py:22

commit v4 on v3

--- a/solution.py
+++ b/solution.py
@@ -135,22 +135,33 @@
     return jnp.where(hit, -jax.nn.sigmoid(-logits), jax.nn.sigmoid(logits)).astype(BF16)
 
 
-def next_kernel(scale, bias, gathered, proj_w, texts, after_out, audio_out):
-    count = after_out.shape[0]
-    audio = normalized(product(gathered[:, 0 : proj_w.shape[0]], proj_w[...]))
+def embedded(pooled, proj_w):
+    return normalized(product(pooled, proj_w[...]))
+
+
+def pulled_by(scale, bias, texts, audio):
+    zt = normalized(texts[texts.shape[0] // 2 :].astype(F32))
+    logits = scale[0] * product(zt, audio, 1) + bias[0]
+    return scale[0] * product(jax.nn.sigmoid(logits).astype(BF16), audio)
+
+
+def next_kernel(scale, bias, *refs):
+    *blocks, proj_w, texts, audio_out, after_out = refs
+    channels = proj_w.shape[0]
+    pooled = jnp.concatenate([block[:, 0:channels] for block in blocks], axis=0)
+    audio = embedded(pooled, proj_w)
     audio_out[...] = audio
-    zt = normalized(texts[count:].astype(F32))
-    logits = scale[0] * product(zt, audio, 1) + bias[0]
-    after_out[...] = (scale[0] * product(jax.nn.sigmoid(logits).astype(BF16), audio)).astype(BF16)
-
-
-def own_kernel(scale, bias, gathered, audio, texts, text_out, pair_out):
-    rows = gathered.shape[0]
-    count = text_out.shape[0]
-    channels = gathered.shape[1] - LANES
+    after_out[...] = pulled_by(scale, bias, texts, audio).astype(BF16)
+
+
+def own_kernel(scale, bias, *refs):
+    *blocks, rows_of, texts, text_out, pair_out = refs
+    count, channels = text_out.shape[0], blocks[0].shape[1] - LANES
+    blk, sub = lax.axis_index("blk"), lax.axis_index("sub")
+    marks = jnp.concatenate([block[:, channels:].astype(F32) for block in blocks], axis=0)
+    rows = marks.shape[0]
     column = rows // 2
-    blk, sub = lax.axis_index("blk"), lax.axis_index("sub")
-    marks = gathered[:, channels : channels + LANES].astype(F32)
+    audio = rows_of[...]
     slot = marks[:, 0:1].astype(jnp.int32)
     match = marks[:, 1:2] + 256.0 * marks[:, 2:3]
     here = lax.broadcasted_iota(jnp.int32, (rows, 1), 0)
@@ -159,35 +170,42 @@
     lane = lax.broadcasted_iota(jnp.int32, (rows, rows), 1)
     picked = lane == source
     near = jnp.concatenate([picked[0:count], picked[column : column + count]], axis=0)
-    pair_out[...] = product(jnp.where(near, 1.0, 0.0).astype(BF16), audio[...]).astype(BF16)
-    wanted_by = jnp.sum(jnp.where(picked, jnp.broadcast_to(match, (rows, rows)), 0.0), 0, keepdims=True)
+    pair_out[...] = product(jnp.where(near, 1.0, 0.0).astype(BF16), audio).astype(BF16)
+    wanted_by = jnp.sum(
+        jnp.where(picked, jnp.broadcast_to(match, (rows, rows)), 0.0), 0, keepdims=True
+    )
     zt = normalized(texts[0:count].astype(F32))
-    logits = scale[0] * product(zt, audio[...], 1) + bias[0]
+    logits = scale[0] * product(zt, audio, 1) + bias[0]
     at = lax.broadcasted_iota(jnp.int32, (count, 1), 0) + (blk * 2 + sub) * count
-    text_out[...] = scale[0] * product(weights(logits, at.astype(F32) == wanted_by), audio[...])
-
-
-def audio_kernel(bits, scale, bias, pair, gathered, texts, peer_out, audio_out):
+    text_out[...] = scale[0] * product(weights(logits, at.astype(F32) == wanted_by), audio)
+
+
+def pushed_by(bits, start, scale, bias, pair, base, opposite, texts):
     count = pair.shape[0] // 2
-    column = gathered.shape[0] // 2
-    channels = gathered.shape[1] - LANES
+    channels = base.shape[1] - LANES
     blk, sub = lax.axis_index("blk"), lax.axis_index("sub")
-    scale, bias = scale[0], bias[0]
     marks = jnp.concatenate(
-        [gathered[0:count, channels:], gathered[column : column + count, channels:]], axis=0
+        [base[0:count, channels:], opposite[0:count, channels:]], axis=0
     ).astype(F32)
     match = marks[:, 1:2] + 256.0 * marks[:, 2:3]
-    zt = normalized(texts[...].astype(F32))
-    logits = scale * product(pair[...], zt, 1) + bias
-    at = lax.broadcasted_iota(jnp.int32, (1, 2 * column), 1)
+    zt = normalized(texts.astype(F32))
+    logits = scale[0] * product(pair[...], zt, 1) + bias[0]
+    at = lax.broadcasted_iota(jnp.int32, (1, texts.shape[0]), 1) + start
     step = at // count
     away = jnp.zeros_like(at)
     for k, bit in enumerate(bits):
         away = away + ((step >> (k + 1)) & 1) * bit
     wanted = jnp.where((step & 1) == 0, ((blk ^ away) * 2 + sub) * count + at % count, -1)
-    pushed = scale * product(weights(logits, wanted.astype(F32) == match), zt)
-    peer_out[...] = pushed[count:].astype(BF16)
-    audio_out[...] = pushed[:count]
+    return scale[0] * product(weights(logits, wanted.astype(F32) == match), zt)
+
+
+def audio_kernel(
+    bits, scale, bias, pair, everyone, texts, peer_out, audio_out
+):
+    count = pair.shape[0] // 2
+    total = pushed_by(bits, 0, scale, bias, pair, everyone, everyone.at[everyone.shape[0] // 2 :], texts[...])
+    peer_out[...] = total[count:].astype(BF16)
+    audio_out[...] = total[:count]
 
 
 def sum_kernel(audio, peer, text, after, audio_grad, text_grad):
@@ -239,58 +257,49 @@
     own, proj_w = tower(clips, lengths, assign, positives, conv_w, proj_w)
     own, both = lax.optimization_barrier((own, jnp.concatenate([text, before], axis=0)))
     gathered = doubled(own, "blk", bits[:-1])
-    gathered, logit_scale, logit_bias = lax.optimization_barrier(
-        (gathered, logit_scale, logit_bias)
+    gathered, later, logit_scale, logit_bias = lax.optimization_barrier(
+        (gathered, both, logit_scale, logit_bias)
     )
     last = bits[-1:]
-    gathered = jnp.concatenate(
-        [
-            gathered,
-            swapped_over(gathered, ("blk",), last),
-            swapped_over(gathered, ("sub",), [1]),
-            swapped_over(gathered, ("blk", "sub"), last + [1]),
-        ],
-        axis=0,
-    )
+    corner = swapped_over(gathered, ("blk", "sub"), last + [1])
+    beside_it = swapped_over(gathered, ("blk",), last)
+    opposite = swapped_over(gathered, ("sub",), [1])
     texts = doubled(both, "blk", bits[:-1])
-    beside = swapped(both, "blk", bits[-1])
-    texts, beside = lax.optimization_barrier((texts, beside))
+    farther = texts[2 * count :]
     texts = jnp.concatenate(
-        [texts, beside, swapped(texts[2 * count :], "blk", bits[-1])], axis=0
-    )
+        [texts, swapped(later, "blk", bits[-1]), swapped(farther, "blk", bits[-1])], axis=0
+    )
+    everyone = jnp.concatenate([gathered, beside_it, opposite, corner], axis=0)
     scale, bias = logit_scale.reshape(1), logit_bias.reshape(1)
-    block = (count, width)
-    after, audio = pl.pallas_call(
-        next_kernel,
-        out_shape=[
-            jax.ShapeDtypeStruct(block, BF16),
-            jax.ShapeDtypeStruct((gathered.shape[0], width), BF16),
-        ],
-        in_specs=[SMEM, SMEM, VMEM, VMEM, VMEM],
-        out_specs=[VMEM] * 2,
-        compiler_params=PARAMS,
-        name="next_texts",
-    )(scale, bias, gathered, proj_w, both)
-    text_part, pair = pl.pallas_call(
-        own_kernel,
-        out_shape=[
-            jax.ShapeDtypeStruct(block, F32),
-            jax.ShapeDtypeStruct((2 * count, width), BF16),
-        ],
-        in_specs=[SMEM, SMEM, VMEM, VMEM, VMEM],
-        out_specs=[VMEM] * 2,
-        compiler_params=PARAMS,
-        name="own_texts",
-    )(scale, bias, gathered, audio, both)
+    block, double = (count, width), (2 * count, width)
+    quarter = gathered.shape[0]
+
+    def call(kernel, name, out_shape, *operands):
+        return pl.pallas_call(
+            kernel,
+            out_shape=[jax.ShapeDtypeStruct(shape, kind) for shape, kind in out_shape],
+            in_specs=[SMEM, SMEM] + [VMEM] * len(operands),
+            out_specs=[VMEM] * len(out_shape),
+            compiler_params=PARAMS,
+            name=name,
+        )(scale, bias, *operands)
+
+    audio, after = call(
+        next_kernel, "next_texts",
+        [((4 * quarter, width), BF16), (block, BF16)],
+        everyone, proj_w, both,
+    )
     after = passed_along(after, "grp", -1)
-    peer, audio_part = pl.pallas_call(
-        functools.partial(audio_kernel, bits),
-        out_shape=[jax.ShapeDtypeStruct(block, t) for t in (BF16, F32)],
-        in_specs=[SMEM, SMEM, VMEM, VMEM, VMEM],
-        out_specs=[VMEM] * 2,
-        compiler_params=PARAMS,
-        name="audio_side",
-    )(scale, bias, pair, gathered, texts)
+    text_part, pair = call(
+        own_kernel, "own_texts",
+        [(block, F32), (double, BF16)],
+        everyone, audio, both,
+    )
+    peer, audio_part = call(
+        functools.partial(audio_kernel, bits), "audio_side",
+        [(block, BF16), (block, F32)],
+        pair, everyone, texts,
+    )
     peer = swapped(peer, "sub", 1)
     return pl.pallas_call(
         sum_kernel,

time: 27.3 us -> 27 us (0.989)
  starting transfers between devices: 13.2 us -> 11.8 us
  waiting for transfers between devices: 5.03 us -> 6.34 us
    ppermute x5, starting transfers between devices: 9.15 us -> 7.73 us  [swapped(): return lax.ppermute(block, axis, [(i, i ^ bit) for i in devices])]
    ppermute x5, waiting for transfers between devices: 2.62 us -> 3.91 us  [swapped(): return lax.ppermute(block, axis, [(i, i ^ bit) for i in devices])]
  transfers between devices with their start and end apart: 10 -> 10, of which waited for: 5 -> 7; matrix products, arithmetic and copies ran while one was open for 0% -> 0% of each run, Pallas kernels for 22% -> 22%
where the time goes in v4:
time: 27 us; the launch traced here: 26.9 us
  starting transfers between devices  11.8 us (44%)
  Pallas kernels  6.7 us (25%)
  waiting for transfers between devices  6.34 us (23%)
  between operations  2.01 us (7%)
    ppermute x5, starting transfers between devices, swapped(): return lax.ppermute(block, axis, [(i, i ^ bit) for i in devices])  7.73 us
    pallas_call x1, Pallas kernels, tower(): pl.pallas_call(tower_kernel, out_shape=[jax.ShapeDtypeStruct((count, chan...  4.25 us
    ppermute x5, waiting for transfers between devices, swapped(): return lax.ppermute(block, axis, [(i, i ^ bit) for i in devices])  3.91 us
    ppermute x3, starting transfers between devices, swapped_over(): return lax.ppermute(block, axes, route)  3.49 us
    ppermute x3, waiting for transfers between devices, swapped_over(): return lax.ppermute(block, axes, route)  2.42 us
    pallas_call x3, Pallas kernels, call(): pl.pallas_call(kernel, out_shape=[jax.ShapeDtypeStruct(shape, kind) for s...  1.79 us
    pallas_call x1, Pallas kernels, on_device(): pl.pallas_call(sum_kernel, out_shape=[jax.ShapeDtypeStruct(block, F32)] *...  0.66 us
    ppermute x2, starting transfers between devices, passed_along(): lax.ppermute(block, axis, [((i - distance) % len(devices), i) for i in de...  0.55 us
  transfers between devices with their start and end apart: 10, of which 7 were waited for; matrix products, arithmetic and copies ran while one was open for 0% of the time, Pallas kernels for 22%

profile of v4, /device:TPU:0, one launch (start us, length us, event | category | flops | bytes accessed | tf_op | source)
XLA Modules:
  0.0 26.9 jit_solution(600463706324630067)
XLA Ops:
  0.6 0.0 copy-start
  0.6 0.5 %collective-permute-start = (bf16[16,1024]{1,0:T(8,128)(2,1)}, bf16[16,1024]{1,0:T(8,128)(2,1)S(1)}, u32[]{:S(2)}, u32[]{:S(2)}) collective-permute-start(bf16[16,1024]{1,0:T(8,128)(2,1)} %param.12), channel_id=1, source_target_pairs={{24,0},{0,8},{8,16},{16,24},{25,1},{1,9},{9,17},{17,25},{26,2},{2,... | collective-permute-start | bytes 98312 | tf_op jit(solution)/shard_map/ppermute | solution.py:39
  1.1 4.2 %tower.1 = (bf16[16,640]{1,0:T(8,128)(2,1)S(1)}, bf16[512,1024]{1,0:T(8,128)(2,1)S(1)}) custom-call(s32[16]{0:T(128)} %lengths_in.1, bf16[16,128,512]{2,1,0:T(8,128)(2,1)} %clips_in.1, s32[1,16]{1,0:T(1,128)} %assign_in.1, s32[1,16]{1,0:T(1,128)} %positives_in.1, bf16[1536,512]{1,0:T(8,128)(2,1)} %conv_in.1, bf16[512,1024]{1,0:T(8,128)(2,1)} %proj_in.1), custom_call_target="tpu_custom_call" | custom-call | flops 1610612736 | bytes 4194304 | tf_op jit(solution)/shard_map/tower/pallas_call | solution.py:223
  5.4 0.0 collective-permute-done
  5.4 0.0 copy-done
  5.4 3.7 %collective-permute-start.1 = (bf16[16,640]{1,0:T(8,128)(2,1)S(1)}, bf16[16,640]{1,0:T(8,128)(2,1)S(1)}, u32[]{:S(2)}, u32[]{:S(2)}) collective-permute-start(bf16[16,640]{1,0:T(8,128)(2,1)S(1)} %get-tuple-element.17), channel_id=1, source_target_pairs={{0,4},{2,6},{4,0},{6,2},{1,5},{3,7},{5,1},{7,3},{8,12},{10,14},{12... | collective-permute-start | bytes 61448 | tf_op jit(solution)/shard_map/ppermute | solution.py:22
  10.4 0.1 collective-permute-start.5
  10.5 0.4 %collective-permute-done.1 = bf16[16,640]{1,0:T(8,128)(2,1)S(1)} collective-permute-done((bf16[16,640]{1,0:T(8,128)(2,1)S(1)}, bf16[16,640]{1,0:T(8,128)(2,1)S(1)}, u32[]{:S(2)}, u32[]{:S(2)}) %collective-permute-start.1) | collective-permute-done | bytes 20512 | tf_op jit(solution)/shard_map/ppermute | solution.py:22
  10.9 1.9 %collective-permute-start.2 = (bf16[32,640]{1,0:T(8,128)(2,1)S(1)}, bf16[32,640]{1,0:T(8,128)(2,1)S(1)}, u32[]{:S(2)}, u32[]{:S(2)}) collective-permute-start(bf16[32,640]{1,0:T(8,128)(2,1)S(1)} %pad_maximum_fusion.2), channel_id=1, source_target_pairs={{0,2},{2,0},{4,6},{6,4},{1,3},{3,1},{5,7},{7,5},{8,10},{10,8},{12,... | collective-permute-start | bytes 122888 | tf_op jit(solution)/shard_map/ppermute | solution.py:34
  12.8 1.5 %collective-permute-start.3 = (bf16[32,640]{1,0:T(8,128)(2,1)S(1)}, bf16[32,640]{1,0:T(8,128)(2,1)S(1)}, u32[]{:S(2)}, u32[]{:S(2)}) collective-permute-start(bf16[32,640]{1,0:T(8,128)(2,1)S(1)} %pad_maximum_fusion.2), channel_id=1, source_target_pairs={{0,1},{1,0},{2,3},{3,2},{4,5},{5,4},{6,7},{7,6},{8,9},{9,8},{10,11... | collective-permute-start | bytes 122888 | tf_op jit(solution)/shard_map/ppermute | solution.py:34
  14.3 0.1 collective-permute-start.4
  14.4 1.9 %collective-permute-start.6 = (bf16[32,1024]{1,0:T(8,128)(2,1)S(1)}, bf16[32,1024]{1,0:T(8,128)(2,1)S(1)}, u32[]{:S(2)}, u32[]{:S(2)}) collective-permute-start(bf16[32,1024]{1,0:T(8,128)(2,1)S(1)} %pad_maximum_fusion.1.refs_2_), channel_id=1, source_target_pairs={{0,2},{2,0},{4,6},{6,4},{1,3},{3,1},{5,7},{7,5},{8,10},{10,8},{12,... | collective-permute-start | bytes 196616 | tf_op jit(solution)/shard_map/ppermute | solution.py:22
  16.3 0.1 collective-permute-done.2
  16.4 0.4 %collective-permute-done.3 = bf16[32,640]{1,0:T(8,128)(2,1)S(1)} collective-permute-done((bf16[32,640]{1,0:T(8,128)(2,1)S(1)}, bf16[32,640]{1,0:T(8,128)(2,1)S(1)}, u32[]{:S(2)}, u32[]{:S(2)}) %collective-permute-start.3) | collective-permute-done | bytes 40992 | tf_op jit(solution)/shard_map/ppermute | solution.py:34
  16.8 0.5 %collective-permute-done.5 = bf16[32,1024]{1,0:T(8,128)(2,1)S(1)} collective-permute-done((bf16[32,1024]{1,0:T(8,128)(2,1)S(1)}, bf16[32,1024]{1,0:T(8,128)(2,1)S(1)}, u32[]{:S(2)}, u32[]{:S(2)}) %collective-permute-start.5) | collective-permute-done | bytes 65568 | tf_op jit(solution)/shard_map/ppermute | solution.py:22
  17.3 0.5 %collective-permute-start.7 = (bf16[32,1024]{1,0:T(8,128)(2,1)S(1)}, bf16[32,1024]{1,0:T(8,128)(2,1)S(1)}, u32[]{:S(2)}, u32[]{:S(2)}) collective-permute-start(bf16[32,1024]{1,0:T(8,128)(2,1)S(1)} %collective-permute-done.5), channel_id=1, source_target_pairs={{0,2},{2,0},{4,6},{6,4},{1,3},{3,1},{5,7},{7,5},{8,10},{10,8},{12,... | collective-permute-start | bytes 196616 | tf_op jit(solution)/shard_map/ppermute | solution.py:22
  17.7 1.9 %collective-permute-done.4 = bf16[32,640]{1,0:T(8,128)(2,1)S(1)} collective-permute-done((bf16[32,640]{1,0:T(8,128)(2,1)S(1)}, bf16[32,640]{1,0:T(8,128)(2,1)S(1)}, u32[]{:S(2)}, u32[]{:S(2)}) %collective-permute-start.4) | collective-permute-done | bytes 40992 | tf_op jit(solution)/shard_map/ppermute | solution.py:34
  19.7 0.8 %next_texts.1 = (bf16[128,1024]{1,0:T(8,128)(2,1)S(1)}, bf16[16,1024]{1,0:T(8,128)(2,1)S(1)}) custom-call(f32[1]{0:T(128)} %bitcast.2.scale, f32[1]{0:T(128)} %bitcast.5.bias, bf16[128,640]{1,0:T(8,128)(2,1)S(1)} %constant_dynamic-update-slice_fusion.refs_0_.everyone, bf16[512,1024]{1,0:T(8,128)(2,1)S(1)} %get-tuple-element.22.refs_1_, ...), custom_call_target="tpu_custom_call" | custom-call | tf_op jit(solution)/shard_map/next_texts/pallas_call | solution.py:278
  20.4 0.0 collective-permute-start.9
  20.5 0.5 %own_texts.1 = (f32[16,1024]{1,0:T(8,128)S(1)}, bf16[32,1024]{1,0:T(8,128)(2,1)S(1)}) custom-call(f32[1]{0:T(128)} %bitcast.3.scale, f32[1]{0:T(128)} %bitcast.6.bias, bf16[128,640]{1,0:T(8,128)(2,1)S(1)} %constant_dynamic-update-slice_fusion.refs_0_.everyone, bf16[128,1024]{1,0:T(8,128)(2,1)S(1)} %get-tuple-element.23.refs_1_, ...), custom_call_target="tpu_custom_call" | custom-call | tf_op jit(solution)/shard_map/own_texts/pallas_call | solution.py:278
  21.0 0.0 collective-permute-done.6
  21.0 0.7 %collective-permute-done.7 = bf16[32,1024]{1,0:T(8,128)(2,1)S(1)} collective-permute-done((bf16[32,1024]{1,0:T(8,128)(2,1)S(1)}, bf16[32,1024]{1,0:T(8,128)(2,1)S(1)}, u32[]{:S(2)}, u32[]{:S(2)}) %collective-permute-start.7) | collective-permute-done | bytes 65568 | tf_op jit(solution)/shard_map/ppermute | solution.py:22
  21.7 0.5 %audio_side.1 = (bf16[16,1024]{1,0:T(8,128)(2,1)S(1)}, f32[16,1024]{1,0:T(8,128)S(1)}) custom-call(f32[1]{0:T(128)} %bitcast.4.scale, f32[1]{0:T(128)} %bitcast.7.bias, bf16[32,1024]{1,0:T(8,128)(2,1)S(1)} %get-tuple-element.24.pair, bf16[128,640]{1,0:T(8,128)(2,1)S(1)} %constant_dynamic-update-slice_fusion.refs_0_.everyone, ...), custom_call_target="tpu_custom_call" | custom-call | tf_op jit(solution)/shard_map/audio_side/pallas_call | solution.py:278
  22.2 1.6 %collective-permute-start.8 = (bf16[16,1024]{1,0:T(8,128)(2,1)S(1)}, bf16[16,1024]{1,0:T(8,128)(2,1)S(1)}, u32[]{:S(2)}, u32[]{:S(2)}) collective-permute-start(bf16[16,1024]{1,0:T(8,128)(2,1)S(1)} %get-tuple-element.27), channel_id=1, source_target_pairs={{0,1},{1,0},{2,3},{3,2},{4,5},{5,4},{6,7},{7,6},{8,9},{9,8},{10,11... | collective-permute-start | bytes 98312 | tf_op jit(solution)/shard_map/ppermute | solution.py:22
  23.8 0.0 collective-permute-done.9.after
  23.8 2.4 %collective-permute-done.8.peer = bf16[16,1024]{1,0:T(8,128)(2,1)S(1)} collective-permute-done((bf16[16,1024]{1,0:T(8,128)(2,1)S(1)}, bf16[16,1024]{1,0:T(8,128)(2,1)S(1)}, u32[]{:S(2)}, u32[]{:S(2)}) %collective-permute-start.8) | collective-permute-done | bytes 32800 | tf_op jit(solution)/shard_map/ppermute | solution.py:22
  26.2 0.7 %sums.1 = (f32[16,1024]{1,0:T(8,128)}, f32[16,1024]{1,0:T(8,128)}) custom-call(f32[16,1024]{1,0:T(8,128)S(1)} %get-tuple-element.26.audio, bf16[16,1024]{1,0:T(8,128)(2,1)S(1)} %collective-permute-done.8.peer, f32[16,1024]{1,0:T(8,128)S(1)} %get-tuple-element.28.text, bf16[16,1024]{1,0:T(8,128)(2,1)S(1)} %collective-permute-done.9.after), custom_call_target="tpu_custom_call" | custom-call | tf_op jit(solution)/shard_map/sums/pallas_call | solution.py:304
  (7 shorter events, 0.1 us)
Async XLA Ops:
  0.6 4.8 %copy-start = (bf16[16,1024]{1,0:T(8,128)(2,1)S(1)}, bf16[16,1024]{1,0:T(8,128)(2,1)}, u32[]{:S(2)}) copy-start(bf16[16,1024]{1,0:T(8,128)(2,1)} %param.12) | copy-start | bytes 98308
  0.6 4.8 %collective-permute-start = (bf16[16,1024]{1,0:T(8,128)(2,1)}, bf16[16,1024]{1,0:T(8,128)(2,1)S(1)}, u32[]{:S(2)}, u32[]{:S(2)}) collective-permute-start(bf16[16,1024]{1,0:T(8,128)(2,1)} %param.12), channel_id=1, source_target_pairs={{24,0},{0,8},{8,16},{16,24},{25,1},{1,9},{9,17},{17,25},{26,2},{2,... | collective-permute-start | bytes 98312 | tf_op jit(solution)/shard_map/ppermute | solution.py:39
  5.4 5.4 %collective-permute-start.1 = (bf16[16,640]{1,0:T(8,128)(2,1)S(1)}, bf16[16,640]{1,0:T(8,128)(2,1)S(1)}, u32[]{:S(2)}, u32[]{:S(2)}) collective-permute-start(bf16[16,640]{1,0:T(8,128)(2,1)S(1)} %get-tuple-element.17), channel_id=1, source_target_pairs={{0,4},{2,6},{4,0},{6,2},{1,5},{3,7},{5,1},{7,3},{8,12},{10,14},{12... | collective-permute-start | bytes 61448 | tf_op jit(solution)/shard_map/ppermute | solution.py:22
  10.4 6.8 %collective-permute-start.5 = (bf16[32,1024]{1,0:T(8,128)(2,1)S(1)}, bf16[32,1024]{1,0:T(8,128)(2,1)S(1)}, u32[]{:S(2)}, u32[]{:S(2)}) collective-permute-start(bf16[32,1024]{1,0:T(8,128)(2,1)S(1)} %pad_maximum_fusion.1.refs_2_), channel_id=1, source_target_pairs={{0,4},{2,6},{4,0},{6,2},{1,5},{3,7},{5,1},{7,3},{8,12},{10,14},{12... | collective-permute-start | bytes 196616 | tf_op jit(solution)/shard_map/ppermute | solution.py:22
  10.9 5.5 %collective-permute-start.2 = (bf16[32,640]{1,0:T(8,128)(2,1)S(1)}, bf16[32,640]{1,0:T(8,128)(2,1)S(1)}, u32[]{:S(2)}, u32[]{:S(2)}) collective-permute-start(bf16[32,640]{1,0:T(8,128)(2,1)S(1)} %pad_maximum_fusion.2), channel_id=1, source_target_pairs={{0,2},{2,0},{4,6},{6,4},{1,3},{3,1},{5,7},{7,5},{8,10},{10,8},{12,... | collective-permute-start | bytes 122888 | tf_op jit(solution)/shard_map/ppermute | solution.py:34
  12.8 4.0 %collective-permute-start.3 = (bf16[32,640]{1,0:T(8,128)(2,1)S(1)}, bf16[32,640]{1,0:T(8,128)(2,1)S(1)}, u32[]{:S(2)}, u32[]{:S(2)}) collective-permute-start(bf16[32,640]{1,0:T(8,128)(2,1)S(1)} %pad_maximum_fusion.2), channel_id=1, source_target_pairs={{0,1},{1,0},{2,3},{3,2},{4,5},{5,4},{6,7},{7,6},{8,9},{9,8},{10,11... | collective-permute-start | bytes 122888 | tf_op jit(solution)/shard_map/ppermute | solution.py:34
  14.3 5.4 %collective-permute-start.4 = (bf16[32,640]{1,0:T(8,128)(2,1)S(1)}, bf16[32,640]{1,0:T(8,128)(2,1)S(1)}, u32[]{:S(2)}, u32[]{:S(2)}) collective-permute-start(bf16[32,640]{1,0:T(8,128)(2,1)S(1)} %pad_maximum_fusion.2), channel_id=1, source_target_pairs={{0,3},{1,2},{2,1},{3,0},{4,7},{5,6},{6,5},{7,4},{8,11},{9,10},{10,... | collective-permute-start | bytes 122888 | tf_op jit(solution)/shard_map/ppermute | solution.py:34
  14.4 6.6 %collective-permute-start.6 = (bf16[32,1024]{1,0:T(8,128)(2,1)S(1)}, bf16[32,1024]{1,0:T(8,128)(2,1)S(1)}, u32[]{:S(2)}, u32[]{:S(2)}) collective-permute-start(bf16[32,1024]{1,0:T(8,128)(2,1)S(1)} %pad_maximum_fusion.1.refs_2_), channel_id=1, source_target_pairs={{0,2},{2,0},{4,6},{6,4},{1,3},{3,1},{5,7},{7,5},{8,10},{10,8},{12,... | collective-permute-start | bytes 196616 | tf_op jit(solution)/shard_map/ppermute | solution.py:22
  17.3 4.4 %collective-permute-start.7 = (bf16[32,1024]{1,0:T(8,128)(2,1)S(1)}, bf16[32,1024]{1,0:T(8,128)(2,1)S(1)}, u32[]{:S(2)}, u32[]{:S(2)}) collective-permute-start(bf16[32,1024]{1,0:T(8,128)(2,1)S(1)} %collective-permute-done.5), channel_id=1, source_target_pairs={{0,2},{2,0},{4,6},{6,4},{1,3},{3,1},{5,7},{7,5},{8,10},{10,8},{12,... | collective-permute-start | bytes 196616 | tf_op jit(solution)/shard_map/ppermute | solution.py:22
  20.4 3.4 %collective-permute-start.9 = (bf16[16,1024]{1,0:T(8,128)(2,1)S(1)}, bf16[16,1024]{1,0:T(8,128)(2,1)S(1)}, u32[]{:S(2)}, u32[]{:S(2)}) collective-permute-start(bf16[16,1024]{1,0:T(8,128)(2,1)S(1)} %get-tuple-element.29), channel_id=1, source_target_pairs={{8,0},{16,8},{24,16},{0,24},{9,1},{17,9},{25,17},{1,25},{10,2},{18... | collective-permute-start | bytes 98312 | tf_op jit(solution)/shard_map/ppermute | solution.py:39
  22.2 4.0 %collective-permute-start.8 = (bf16[16,1024]{1,0:T(8,128)(2,1)S(1)}, bf16[16,1024]{1,0:T(8,128)(2,1)S(1)}, u32[]{:S(2)}, u32[]{:S(2)}) collective-permute-start(bf16[16,1024]{1,0:T(8,128)(2,1)S(1)} %get-tuple-element.27), channel_id=1, source_target_pairs={{0,1},{1,0},{2,3},{3,2},{4,5},{5,4},{6,7},{7,6},{8,9},{9,8},{10,11... | collective-permute-start | bytes 98312 | tf_op jit(solution)/shard_map/ppermute | solution.py:22

commit v5 on v4

--- a/solution.py
+++ b/solution.py
@@ -51,7 +51,8 @@
 
 
 def gelu(x):
-    return x * (0.5 + 0.5 * jnp.tanh(x * (0.7978845608028654 + 0.035677408136300125 * (x * x))))
+    x = x.astype(BF16)
+    return (x * (BF16(0.5) + BF16(0.5) * jnp.tanh(x * (BF16(0.7978845608028654) + BF16(0.035677408136300125) * (x * x))))).astype(F32)
 
 
 def as_column(row):

time: 27 us -> 26.9 us (level)
  waiting for transfers between devices: 6.34 us -> 5.93 us
  starting transfers between devices: 11.8 us -> 12.2 us
    ppermute x5, waiting for transfers between devices: 3.91 us -> 3.44 us  [swapped(): return lax.ppermute(block, axis, [(i, i ^ bit) for i in devices])]
    ppermute x5, starting transfers between devices: 7.73 us -> 8.15 us  [swapped(): return lax.ppermute(block, axis, [(i, i ^ bit) for i in devices])]
  transfers between devices with their start and end apart: 10 -> 10, of which waited for: 7 -> 5; matrix products, arithmetic and copies ran while one was open for 0% -> 0% of each run, Pallas kernels for 22% -> 22%
where the time goes in v5:
time: 26.9 us; the launch traced here: 26.7 us
  starting transfers between devices  12.2 us (45%)
  Pallas kernels  6.5 us (24%)
  waiting for transfers between devices  5.93 us (22%)
  between operations  2.01 us (7%)
    ppermute x5, starting transfers between devices, swapped(): return lax.ppermute(block, axis, [(i, i ^ bit) for i in devices])  8.15 us
    pallas_call x1, Pallas kernels, tower(): pl.pallas_call(tower_kernel, out_shape=[jax.ShapeDtypeStruct((count, chan...  4.05 us
    ppermute x3, starting transfers between devices, swapped_over(): return lax.ppermute(block, axes, route)  3.49 us
    ppermute x5, waiting for transfers between devices, swapped(): return lax.ppermute(block, axis, [(i, i ^ bit) for i in devices])  3.44 us
    ppermute x3, waiting for transfers between devices, swapped_over(): return lax.ppermute(block, axes, route)  2.48 us
    pallas_call x3, Pallas kernels, call(): pl.pallas_call(kernel, out_shape=[jax.ShapeDtypeStruct(shape, kind) for s...  1.79 us
    pallas_call x1, Pallas kernels, on_device(): pl.pallas_call(sum_kernel, out_shape=[jax.ShapeDtypeStruct(block, F32)] *...  0.66 us
    ppermute x2, starting transfers between devices, passed_along(): lax.ppermute(block, axis, [((i - distance) % len(devices), i) for i in de...  0.55 us
  transfers between devices with their start and end apart: 10, of which 5 were waited for; matrix products, arithmetic and copies ran while one was open for 0% of the time, Pallas kernels for 22%

profile of v5, /device:TPU:0, one launch (start us, length us, event | category | flops | bytes accessed | tf_op | source)
XLA Modules:
  0.0 26.7 jit_solution(13365592187676447006)
XLA Ops:
  0.6 0.0 copy-start
  0.6 0.5 %collective-permute-start = (bf16[16,1024]{1,0:T(8,128)(2,1)}, bf16[16,1024]{1,0:T(8,128)(2,1)S(1)}, u32[]{:S(2)}, u32[]{:S(2)}) collective-permute-start(bf16[16,1024]{1,0:T(8,128)(2,1)} %param.12), channel_id=1, source_target_pairs={{24,0},{0,8},{8,16},{16,24},{25,1},{1,9},{9,17},{17,25},{26,2},{2,... | collective-permute-start | bytes 98312 | tf_op jit(solution)/shard_map/ppermute | solution.py:39
  1.1 4.1 %tower.1 = (bf16[16,640]{1,0:T(8,128)(2,1)S(1)}, bf16[512,1024]{1,0:T(8,128)(2,1)S(1)}) custom-call(s32[16]{0:T(128)} %lengths_in.1, bf16[16,128,512]{2,1,0:T(8,128)(2,1)} %clips_in.1, s32[1,16]{1,0:T(1,128)} %assign_in.1, s32[1,16]{1,0:T(1,128)} %positives_in.1, bf16[1536,512]{1,0:T(8,128)(2,1)} %conv_in.1, bf16[512,1024]{1,0:T(8,128)(2,1)} %proj_in.1), custom_call_target="tpu_custom_call" | custom-call | flops 1610612736 | bytes 4194304 | tf_op jit(solution)/shard_map/tower/pallas_call | solution.py:224
  5.2 0.0 collective-permute-done
  5.2 0.0 copy-done
  5.2 3.7 %collective-permute-start.1 = (bf16[16,640]{1,0:T(8,128)(2,1)S(1)}, bf16[16,640]{1,0:T(8,128)(2,1)S(1)}, u32[]{:S(2)}, u32[]{:S(2)}) collective-permute-start(bf16[16,640]{1,0:T(8,128)(2,1)S(1)} %get-tuple-element.17), channel_id=1, source_target_pairs={{0,4},{2,6},{4,0},{6,2},{1,5},{3,7},{5,1},{7,3},{8,12},{10,14},{12... | collective-permute-start | bytes 61448 | tf_op jit(solution)/shard_map/ppermute | solution.py:22
  10.2 0.1 collective-permute-start.5
  10.3 0.4 %collective-permute-done.1 = bf16[16,640]{1,0:T(8,128)(2,1)S(1)} collective-permute-done((bf16[16,640]{1,0:T(8,128)(2,1)S(1)}, bf16[16,640]{1,0:T(8,128)(2,1)S(1)}, u32[]{:S(2)}, u32[]{:S(2)}) %collective-permute-start.1) | collective-permute-done | bytes 20512 | tf_op jit(solution)/shard_map/ppermute | solution.py:22
  10.7 1.9 %collective-permute-start.2 = (bf16[32,640]{1,0:T(8,128)(2,1)S(1)}, bf16[32,640]{1,0:T(8,128)(2,1)S(1)}, u32[]{:S(2)}, u32[]{:S(2)}) collective-permute-start(bf16[32,640]{1,0:T(8,128)(2,1)S(1)} %pad_maximum_fusion.2), channel_id=1, source_target_pairs={{0,2},{2,0},{4,6},{6,4},{1,3},{3,1},{5,7},{7,5},{8,10},{10,8},{12,... | collective-permute-start | bytes 122888 | tf_op jit(solution)/shard_map/ppermute | solution.py:34
  12.6 1.5 %collective-permute-start.3 = (bf16[32,640]{1,0:T(8,128)(2,1)S(1)}, bf16[32,640]{1,0:T(8,128)(2,1)S(1)}, u32[]{:S(2)}, u32[]{:S(2)}) collective-permute-start(bf16[32,640]{1,0:T(8,128)(2,1)S(1)} %pad_maximum_fusion.2), channel_id=1, source_target_pairs={{0,1},{1,0},{2,3},{3,2},{4,5},{5,4},{6,7},{7,6},{8,9},{9,8},{10,11... | collective-permute-start | bytes 122888 | tf_op jit(solution)/shard_map/ppermute | solution.py:34
  14.1 0.1 collective-permute-start.4
  14.2 1.9 %collective-permute-start.6 = (bf16[32,1024]{1,0:T(8,128)(2,1)S(1)}, bf16[32,1024]{1,0:T(8,128)(2,1)S(1)}, u32[]{:S(2)}, u32[]{:S(2)}) collective-permute-start(bf16[32,1024]{1,0:T(8,128)(2,1)S(1)} %pad_maximum_fusion.1.refs_2_), channel_id=1, source_target_pairs={{0,2},{2,0},{4,6},{6,4},{1,3},{3,1},{5,7},{7,5},{8,10},{10,8},{12,... | collective-permute-start | bytes 196616 | tf_op jit(solution)/shard_map/ppermute | solution.py:22
  16.1 0.0 collective-permute-done.2
  16.1 0.5 %collective-permute-done.3 = bf16[32,640]{1,0:T(8,128)(2,1)S(1)} collective-permute-done((bf16[32,640]{1,0:T(8,128)(2,1)S(1)}, bf16[32,640]{1,0:T(8,128)(2,1)S(1)}, u32[]{:S(2)}, u32[]{:S(2)}) %collective-permute-start.3) | collective-permute-done | bytes 40992 | tf_op jit(solution)/shard_map/ppermute | solution.py:34
  16.6 0.0 collective-permute-done.5
  16.6 0.9 %collective-permute-start.7 = (bf16[32,1024]{1,0:T(8,128)(2,1)S(1)}, bf16[32,1024]{1,0:T(8,128)(2,1)S(1)}, u32[]{:S(2)}, u32[]{:S(2)}) collective-permute-start(bf16[32,1024]{1,0:T(8,128)(2,1)S(1)} %collective-permute-done.5), channel_id=1, source_target_pairs={{0,2},{2,0},{4,6},{6,4},{1,3},{3,1},{5,7},{7,5},{8,10},{10,8},{12,... | collective-permute-start | bytes 196616 | tf_op jit(solution)/shard_map/ppermute | solution.py:22
  17.5 2.0 %collective-permute-done.4 = bf16[32,640]{1,0:T(8,128)(2,1)S(1)} collective-permute-done((bf16[32,640]{1,0:T(8,128)(2,1)S(1)}, bf16[32,640]{1,0:T(8,128)(2,1)S(1)}, u32[]{:S(2)}, u32[]{:S(2)}) %collective-permute-start.4) | collective-permute-done | bytes 40992 | tf_op jit(solution)/shard_map/ppermute | solution.py:34
  19.5 0.8 %next_texts.1 = (bf16[128,1024]{1,0:T(8,128)(2,1)S(1)}, bf16[16,1024]{1,0:T(8,128)(2,1)S(1)}) custom-call(f32[1]{0:T(128)} %bitcast.2.scale, f32[1]{0:T(128)} %bitcast.5.bias, bf16[128,640]{1,0:T(8,128)(2,1)S(1)} %constant_dynamic-update-slice_fusion.refs_0_.everyone, bf16[512,1024]{1,0:T(8,128)(2,1)S(1)} %get-tuple-element.22.refs_1_, ...), custom_call_target="tpu_custom_call" | custom-call | tf_op jit(solution)/shard_map/next_texts/pallas_call | solution.py:279
  20.2 0.0 collective-permute-start.9
  20.3 0.5 %own_texts.1 = (f32[16,1024]{1,0:T(8,128)S(1)}, bf16[32,1024]{1,0:T(8,128)(2,1)S(1)}) custom-call(f32[1]{0:T(128)} %bitcast.3.scale, f32[1]{0:T(128)} %bitcast.6.bias, bf16[128,640]{1,0:T(8,128)(2,1)S(1)} %constant_dynamic-update-slice_fusion.refs_0_.everyone, bf16[128,1024]{1,0:T(8,128)(2,1)S(1)} %get-tuple-element.23.refs_1_, ...), custom_call_target="tpu_custom_call" | custom-call | tf_op jit(solution)/shard_map/own_texts/pallas_call | solution.py:279
  20.8 0.0 collective-permute-done.6
  20.8 0.7 %collective-permute-done.7 = bf16[32,1024]{1,0:T(8,128)(2,1)S(1)} collective-permute-done((bf16[32,1024]{1,0:T(8,128)(2,1)S(1)}, bf16[32,1024]{1,0:T(8,128)(2,1)S(1)}, u32[]{:S(2)}, u32[]{:S(2)}) %collective-permute-start.7) | collective-permute-done | bytes 65568 | tf_op jit(solution)/shard_map/ppermute | solution.py:22
  21.5 0.5 %audio_side.1 = (bf16[16,1024]{1,0:T(8,128)(2,1)S(1)}, f32[16,1024]{1,0:T(8,128)S(1)}) custom-call(f32[1]{0:T(128)} %bitcast.4.scale, f32[1]{0:T(128)} %bitcast.7.bias, bf16[32,1024]{1,0:T(8,128)(2,1)S(1)} %get-tuple-element.24.pair, bf16[128,640]{1,0:T(8,128)(2,1)S(1)} %constant_dynamic-update-slice_fusion.refs_0_.everyone, ...), custom_call_target="tpu_custom_call" | custom-call | tf_op jit(solution)/shard_map/audio_side/pallas_call | solution.py:279
  22.1 1.6 %collective-permute-start.8 = (bf16[16,1024]{1,0:T(8,128)(2,1)S(1)}, bf16[16,1024]{1,0:T(8,128)(2,1)S(1)}, u32[]{:S(2)}, u32[]{:S(2)}) collective-permute-start(bf16[16,1024]{1,0:T(8,128)(2,1)S(1)} %get-tuple-element.27), channel_id=1, source_target_pairs={{0,1},{1,0},{2,3},{3,2},{4,5},{5,4},{6,7},{7,6},{8,9},{9,8},{10,11... | collective-permute-start | bytes 98312 | tf_op jit(solution)/shard_map/ppermute | solution.py:22
  23.7 0.0 collective-permute-done.9.after
  23.7 2.3 %collective-permute-done.8.peer = bf16[16,1024]{1,0:T(8,128)(2,1)S(1)} collective-permute-done((bf16[16,1024]{1,0:T(8,128)(2,1)S(1)}, bf16[16,1024]{1,0:T(8,128)(2,1)S(1)}, u32[]{:S(2)}, u32[]{:S(2)}) %collective-permute-start.8) | collective-permute-done | bytes 32800 | tf_op jit(solution)/shard_map/ppermute | solution.py:22
  26.0 0.7 %sums.1 = (f32[16,1024]{1,0:T(8,128)}, f32[16,1024]{1,0:T(8,128)}) custom-call(f32[16,1024]{1,0:T(8,128)S(1)} %get-tuple-element.26.audio, bf16[16,1024]{1,0:T(8,128)(2,1)S(1)} %collective-permute-done.8.peer, f32[16,1024]{1,0:T(8,128)S(1)} %get-tuple-element.28.text, bf16[16,1024]{1,0:T(8,128)(2,1)S(1)} %collective-permute-done.9.after), custom_call_target="tpu_custom_call" | custom-call | tf_op jit(solution)/shard_map/sums/pallas_call | solution.py:305
  (7 shorter events, 0.1 us)
Async XLA Ops:
  0.6 4.6 %copy-start = (bf16[16,1024]{1,0:T(8,128)(2,1)S(1)}, bf16[16,1024]{1,0:T(8,128)(2,1)}, u32[]{:S(2)}) copy-start(bf16[16,1024]{1,0:T(8,128)(2,1)} %param.12) | copy-start | bytes 98308
  0.6 4.6 %collective-permute-start = (bf16[16,1024]{1,0:T(8,128)(2,1)}, bf16[16,1024]{1,0:T(8,128)(2,1)S(1)}, u32[]{:S(2)}, u32[]{:S(2)}) collective-permute-start(bf16[16,1024]{1,0:T(8,128)(2,1)} %param.12), channel_id=1, source_target_pairs={{24,0},{0,8},{8,16},{16,24},{25,1},{1,9},{9,17},{17,25},{26,2},{2,... | collective-permute-start | bytes 98312 | tf_op jit(solution)/shard_map/ppermute | solution.py:39
  5.2 5.4 %collective-permute-start.1 = (bf16[16,640]{1,0:T(8,128)(2,1)S(1)}, bf16[16,640]{1,0:T(8,128)(2,1)S(1)}, u32[]{:S(2)}, u32[]{:S(2)}) collective-permute-start(bf16[16,640]{1,0:T(8,128)(2,1)S(1)} %get-tuple-element.17), channel_id=1, source_target_pairs={{0,4},{2,6},{4,0},{6,2},{1,5},{3,7},{5,1},{7,3},{8,12},{10,14},{12... | collective-permute-start | bytes 61448 | tf_op jit(solution)/shard_map/ppermute | solution.py:22
  10.2 6.4 %collective-permute-start.5 = (bf16[32,1024]{1,0:T(8,128)(2,1)S(1)}, bf16[32,1024]{1,0:T(8,128)(2,1)S(1)}, u32[]{:S(2)}, u32[]{:S(2)}) collective-permute-start(bf16[32,1024]{1,0:T(8,128)(2,1)S(1)} %pad_maximum_fusion.1.refs_2_), channel_id=1, source_target_pairs={{0,4},{2,6},{4,0},{6,2},{1,5},{3,7},{5,1},{7,3},{8,12},{10,14},{12... | collective-permute-start | bytes 196616 | tf_op jit(solution)/shard_map/ppermute | solution.py:22
  10.7 5.4 %collective-permute-start.2 = (bf16[32,640]{1,0:T(8,128)(2,1)S(1)}, bf16[32,640]{1,0:T(8,128)(2,1)S(1)}, u32[]{:S(2)}, u32[]{:S(2)}) collective-permute-start(bf16[32,640]{1,0:T(8,128)(2,1)S(1)} %pad_maximum_fusion.2), channel_id=1, source_target_pairs={{0,2},{2,0},{4,6},{6,4},{1,3},{3,1},{5,7},{7,5},{8,10},{10,8},{12,... | collective-permute-start | bytes 122888 | tf_op jit(solution)/shard_map/ppermute | solution.py:34
  12.6 4.0 %collective-permute-start.3 = (bf16[32,640]{1,0:T(8,128)(2,1)S(1)}, bf16[32,640]{1,0:T(8,128)(2,1)S(1)}, u32[]{:S(2)}, u32[]{:S(2)}) collective-permute-start(bf16[32,640]{1,0:T(8,128)(2,1)S(1)} %pad_maximum_fusion.2), channel_id=1, source_target_pairs={{0,1},{1,0},{2,3},{3,2},{4,5},{5,4},{6,7},{7,6},{8,9},{9,8},{10,11... | collective-permute-start | bytes 122888 | tf_op jit(solution)/shard_map/ppermute | solution.py:34
  14.1 5.3 %collective-permute-start.4 = (bf16[32,640]{1,0:T(8,128)(2,1)S(1)}, bf16[32,640]{1,0:T(8,128)(2,1)S(1)}, u32[]{:S(2)}, u32[]{:S(2)}) collective-permute-start(bf16[32,640]{1,0:T(8,128)(2,1)S(1)} %pad_maximum_fusion.2), channel_id=1, source_target_pairs={{0,3},{1,2},{2,1},{3,0},{4,7},{5,6},{6,5},{7,4},{8,11},{9,10},{10,... | collective-permute-start | bytes 122888 | tf_op jit(solution)/shard_map/ppermute | solution.py:34
  14.2 6.6 %collective-permute-start.6 = (bf16[32,1024]{1,0:T(8,128)(2,1)S(1)}, bf16[32,1024]{1,0:T(8,128)(2,1)S(1)}, u32[]{:S(2)}, u32[]{:S(2)}) collective-permute-start(bf16[32,1024]{1,0:T(8,128)(2,1)S(1)} %pad_maximum_fusion.1.refs_2_), channel_id=1, source_target_pairs={{0,2},{2,0},{4,6},{6,4},{1,3},{3,1},{5,7},{7,5},{8,10},{10,8},{12,... | collective-permute-start | bytes 196616 | tf_op jit(solution)/shard_map/ppermute | solution.py:22
  16.6 4.9 %collective-permute-start.7 = (bf16[32,1024]{1,0:T(8,128)(2,1)S(1)}, bf16[32,1024]{1,0:T(8,128)(2,1)S(1)}, u32[]{:S(2)}, u32[]{:S(2)}) collective-permute-start(bf16[32,1024]{1,0:T(8,128)(2,1)S(1)} %collective-permute-done.5), channel_id=1, source_target_pairs={{0,2},{2,0},{4,6},{6,4},{1,3},{3,1},{5,7},{7,5},{8,10},{10,8},{12,... | collective-permute-start | bytes 196616 | tf_op jit(solution)/shard_map/ppermute | solution.py:22
  20.2 3.5 %collective-permute-start.9 = (bf16[16,1024]{1,0:T(8,128)(2,1)S(1)}, bf16[16,1024]{1,0:T(8,128)(2,1)S(1)}, u32[]{:S(2)}, u32[]{:S(2)}) collective-permute-start(bf16[16,1024]{1,0:T(8,128)(2,1)S(1)} %get-tuple-element.29), channel_id=1, source_target_pairs={{8,0},{16,8},{24,16},{0,24},{9,1},{17,9},{25,17},{1,25},{10,2},{18... | collective-permute-start | bytes 98312 | tf_op jit(solution)/shard_map/ppermute | solution.py:39
  22.1 4.0 %collective-permute-start.8 = (bf16[16,1024]{1,0:T(8,128)(2,1)S(1)}, bf16[16,1024]{1,0:T(8,128)(2,1)S(1)}, u32[]{:S(2)}, u32[]{:S(2)}) collective-permute-start(bf16[16,1024]{1,0:T(8,128)(2,1)S(1)} %get-tuple-element.27), channel_id=1, source_target_pairs={{0,1},{1,0},{2,3},{3,2},{4,5},{5,4},{6,7},{7,6},{8,9},{9,8},{10,11... | collective-permute-start | bytes 98312 | tf_op jit(solution)/shard_map/ppermute | solution.py:22
